TPU v7x, 512 devices: a whole 4x4x16 slice. The times are simulated.
512 devices in a mesh: branch: 2 (over z_hi), seq: 32 (over y, z_lo), head: 8 (over x, core).
Axes of the slice: x: 4, y: 4, z: 16 (z_hi: 2, z_lo: 8; z = z_hi * 8 + z_lo), core: 2. Of those that a mesh axis runs over, the one named last changes fastest.
Arguments:
- query_proj: bfloat16 [2, 4096, 3072], P('branch', 'seq', 'head'), may hold values from -120 to 120
- key_proj: bfloat16 [2, 4096, 3072], P('branch', 'seq', 'head'), may hold values from -4 to 4
- value_proj: bfloat16 [2, 4096, 3072], P('branch', 'seq', 'head'), may hold values from -6 to 6
- out_weight: bfloat16 [3072, 3072], P('head'), may hold values from -6 to 6
Outputs:
- projected: bfloat16 [2, 4096, 3072], P('branch', 'seq', 'head')
All inputs are finite; a program needn't handle non-finite values.
Results may differ from a plain program's by a relative error of at most 0.02.
Values may be sent and summed in bfloat16 or wider, within the bound.
No kernel may reach another device: no remote copies, remote signals or barrier semaphores. Data moves between devices by JAX's collectives and lax.ppermute only.
A program may use at most 64 MiB of HBM per device.

v0:
```python
import math

import jax
import jax.numpy as jnp
from jax import lax
from jax.sharding import PartitionSpec as P

DH = 128


def from_behind(value, axis, steps):
    count = lax.axis_size(axis)
    first, last = (max(0, -steps), min(count, count - steps))
    return lax.ppermute(value, axis, [(source, source + steps) for source in range(first, last)])


def start_state(head_count, tok_rows):
    return (
        jnp.full((head_count, tok_rows), -jnp.inf, jnp.float32),
        jnp.zeros((head_count, tok_rows), jnp.float32),
        jnp.zeros((head_count, tok_rows, DH), jnp.float32),
    )


def attend_piece(state_in, block_in, query_heads):
    row_peak, row_total, row_accum = state_in
    key_block, value_block = block_in
    block_len = key_block.shape[1]
    head_count = query_heads.shape[1]
    key_heads = key_block[0].reshape(block_len, head_count, DH)
    value_heads = value_block[0].reshape(block_len, head_count, DH)
    scores = jnp.einsum(
        "rhd,nhd->hrn", query_heads, key_heads, preferred_element_type=jnp.float32
    ) * (1.0 / math.sqrt(DH))
    new_peak = jnp.max(scores, axis=2)
    rescale = jnp.exp(row_peak - new_peak)
    weights = jnp.exp(scores - new_peak[:, :, None])
    new_total = row_total * rescale + jnp.sum(weights, axis=2)
    product = jnp.einsum(
        "hrn,nhd->hrd",
        weights.astype(jnp.bfloat16),
        value_heads,
        preferred_element_type=jnp.float32,
    )
    return (new_peak, new_total, row_accum * rescale[:, :, None] + product)


def body(query_proj, key_proj, value_proj, out_weight):
    tok_rows = query_proj.shape[1]
    feat_width = query_proj.shape[2]
    head_count = feat_width // DH
    own_queries = query_proj[0].reshape(tok_rows, head_count, DH)

    def own_step(state_in, block_in):
        return attend_piece(state_in, block_in, own_queries)

    partner = from_behind((key_proj, value_proj), "branch", 1)
    own_state = own_step(
        start_state(head_count, tok_rows),
        (
            lax.all_gather(key_proj, "seq", axis=1, tiled=True),
            lax.all_gather(value_proj, "seq", axis=1, tiled=True),
        ),
    )
    cross_state = own_step(
        start_state(head_count, tok_rows),
        (
            lax.all_gather(partner[0], "seq", axis=1, tiled=True),
            lax.all_gather(partner[1], "seq", axis=1, tiled=True),
        ),
    )
    is_edit = lax.axis_index("branch") == 1
    cross_peak = jnp.where(is_edit, cross_state[0], -jnp.inf)
    merged_peak = jnp.maximum(own_state[0], cross_peak)
    own_factor = jnp.exp(own_state[0] - merged_peak)
    cross_factor = jnp.exp(cross_peak - merged_peak)
    merged_total = own_state[1] * own_factor + cross_state[1] * cross_factor
    merged_accum = own_state[2] * own_factor[:, :, None] + cross_state[2] * cross_factor[:, :, None]
    attended = (merged_accum / merged_total[:, :, None]).astype(jnp.bfloat16)
    attended = attended.transpose(1, 0, 2).reshape(tok_rows, feat_width)
    partial_out = jnp.dot(attended, out_weight, preferred_element_type=jnp.float32)
    summed = lax.psum_scatter(
        partial_out.astype(jnp.bfloat16), "head", scatter_dimension=1, tiled=True
    )
    return summed[None]


def solution(mesh):
    placed = (
        P("branch", "seq", "head"),
        P("branch", "seq", "head"),
        P("branch", "seq", "head"),
        P("head", None),
    )
    return jax.shard_map(
        body, mesh=mesh, in_specs=placed, out_specs=P("branch", "seq", "head"), check_vma=False
    )
```

profile of v0, /device:TPU:1, one launch (start us, length us, event | category | flops | bytes accessed | tf_op | source)
XLA Modules:
  0.0 931.4 jit_solution(6311393911980643641)
XLA Ops:
  6.5 0.7 all-gather.7.cloned.1.call-update
  7.3 0.0 all-gather.5.cloned.1.call-start
  7.3 1.6 copy.19
  8.9 0.0 all-gather.5.cloned.1.call-update
  9.0 0.0 all-gather.9.cloned.1.call-start
  9.0 16.3 %collective-permute-start = (bf16[1,128,384]{1,2,0:T(8,128)(2,1)}, bf16[1,128,384]{1,2,0:T(8,128)(2,1)S(1)}, u32[]{:S(2)}, u32[]{:S(2)}) collective-permute-start(bf16[1,128,384]{1,2,0:T(8,128)(2,1)} %copy.19), channel_id=1, source_target_pairs={{0,256},{1,257},{2,258},{3,259},{4,260},{5,261},{6,262},{7,263},{8... | collective-permute-start | bytes 294920 | tf_op jit(solution)/shard_map/ppermute | solution.py:14
  25.3 1.9 collective-permute-done
  27.2 0.6 copy-done.5
  27.9 0.0 all-gather.11.cloned.1.call-start
  27.9 12.6 %collective-permute-start.1 = (bf16[1,128,384]{2,1,0:T(8,128)(2,1)}, bf16[1,128,384]{2,1,0:T(8,128)(2,1)S(1)}, u32[]{:S(2)}, u32[]{:S(2)}) collective-permute-start(bf16[1,128,384]{2,1,0:T(8,128)(2,1)} %param.6), channel_id=1, source_target_pairs={{0,256},{1,257},{2,258},{3,259},{4,260},{5,261},{6,262},{7,263},{8... | collective-permute-start | bytes 294920 | tf_op jit(solution)/shard_map/ppermute | solution.py:14
  40.5 1.9 collective-permute-done.1
  42.4 0.6 copy-done.4
  43.1 0.0 reduce-scatter.4.cloned.1.call-start
  43.2 1.0 copy.18
  44.2 184.1 %all-gather.7.cloned.1.call-done = bf16[1,4096,384]{2,1,0:T(8,128)(2,1)} async-done(((bf16[1,128,384]{2,1,0:T(8,128)(2,1)}), bf16[1,4096,384]{2,1,0:T(8,128)(2,1)}) %all-gather.7.cloned.1.call-update) | async-done | bytes 3145744 | tf_op jit(solution)/shard_map/all_gather | solution.py:62
  228.3 4.7 copy.22
  232.9 200.1 %all-gather.5.cloned.1.call-done = bf16[1,4096,384]{1,2,0:T(8,128)(2,1)} async-done(((bf16[1,128,384]{1,2,0:T(8,128)(2,1)}), bf16[1,4096,384]{1,2,0:T(8,128)(2,1)}) %all-gather.5.cloned.1.call-update) | async-done | bytes 3145744 | tf_op jit(solution)/shard_map/all_gather | solution.py:61
  433.0 5.6 fusion.46
  438.6 191.9 %all-gather.9.cloned.1.call-done = bf16[1,4096,384]{1,2,0:T(8,128)(2,1)} async-done(((bf16[1,128,384]{1,2,0:T(8,128)(2,1)}), bf16[1,4096,384]{1,2,0:T(8,128)(2,1)}) %all-gather.9.cloned.1.call-update) | async-done | bytes 3145744 | tf_op jit(solution)/shard_map/all_gather | solution.py:68
  630.6 3.2 fusion.47
  633.8 0.5 copy-done.1
  634.3 2.0 fusion
  636.3 0.5 copy-done.2
  636.7 1.2 copy-done.3
  637.9 1.3 fusion.28
  639.2 217.3 %all-gather.11.cloned.1.call-done = bf16[1,4096,384]{2,1,0:T(8,128)(2,1)} async-done(((bf16[1,128,384]{2,1,0:T(8,128)(2,1)}), bf16[1,4096,384]{2,1,0:T(8,128)(2,1)}) %all-gather.11.cloned.1.call-update) | async-done | bytes 3145744 | tf_op jit(solution)/shard_map/all_gather | solution.py:69
  856.6 4.8 copy.26
  861.3 4.9 fusion.34
  866.3 0.6 convolution_convert_fusion
  866.9 1.2 copy.31
  868.1 55.2 %reduce-scatter.4.cloned.1.call-done = bf16[384,128]{1,0:T(8,128)(2,1)} async-done(((bf16[3072,128]{1,0:T(8,128)(2,1)}), bf16[384,128]{1,0:T(8,128)(2,1)}) %reduce-scatter.4.cloned.1.call-update) | async-done | bytes 98320
  923.3 1.6 copy.32
  (13 shorter events, 0.1 us)
Async XLA Ops:
  6.5 859.7 %copy-start = (bf16[384,3072]{1,0:T(8,128)(2,1)S(1)}, bf16[384,3072]{1,0:T(8,128)(2,1)}, u32[]{:S(2)}) copy-start(bf16[384,3072]{1,0:T(8,128)(2,1)} %param.7) | copy-start | bytes 7077892
  6.5 221.8 %all-gather.7.cloned.1.call-start = ((), (), s32[]{:S(2)}) async-start(), calls=%async_computation.2 | async-start | bytes 3244032 | tf_op jit(solution)/shard_map/all_gather | solution.py:62
  7.3 425.7 %all-gather.5.cloned.1.call-start = ((), (), s32[]{:S(2)}) async-start(), calls=%async_computation.1 | async-start | bytes 3244032 | tf_op jit(solution)/shard_map/all_gather | solution.py:61
  9.0 621.6 %all-gather.9.cloned.1.call-start = ((), (), s32[]{:S(2)}) async-start(), calls=%async_computation.3 | async-start | bytes 3244032 | tf_op jit(solution)/shard_map/all_gather | solution.py:68
  9.0 18.2 %collective-permute-start = (bf16[1,128,384]{1,2,0:T(8,128)(2,1)}, bf16[1,128,384]{1,2,0:T(8,128)(2,1)S(1)}, u32[]{:S(2)}, u32[]{:S(2)}) collective-permute-start(bf16[1,128,384]{1,2,0:T(8,128)(2,1)} %copy.19), channel_id=1, source_target_pairs={{0,256},{1,257},{2,258},{3,259},{4,260},{5,261},{6,262},{7,263},{8... | collective-permute-start | bytes 294920 | tf_op jit(solution)/shard_map/ppermute | solution.py:14
  27.2 0.6 copy-start.5
  27.9 828.7 %all-gather.11.cloned.1.call-start = ((), (), s32[]{:S(2)}) async-start(), calls=%async_computation.4 | async-start | bytes 3244032 | tf_op jit(solution)/shard_map/all_gather | solution.py:69
  27.9 14.5 %collective-permute-start.1 = (bf16[1,128,384]{2,1,0:T(8,128)(2,1)}, bf16[1,128,384]{2,1,0:T(8,128)(2,1)S(1)}, u32[]{:S(2)}, u32[]{:S(2)}) collective-permute-start(bf16[1,128,384]{2,1,0:T(8,128)(2,1)} %param.6), channel_id=1, source_target_pairs={{0,256},{1,257},{2,258},{3,259},{4,260},{5,261},{6,262},{7,263},{8... | collective-permute-start | bytes 294920 | tf_op jit(solution)/shard_map/ppermute | solution.py:14
  42.4 0.6 copy-start.4
  43.1 880.2 %reduce-scatter.4.cloned.1.call-start = ((), (), s32[]{:S(2)}) async-start(), calls=%async_computation.5 | async-start | bytes 884736
  630.6 3.7 copy-start.1
  633.8 2.9 copy-start.2
  634.3 3.6 copy-start.3
Sparse Core Ops, SparseCore 0:
  9.4 218.8 all-gather.6
  230.3 202.6 all-gather.4
  435.0 195.5 all-gather.8
  632.5 224.0 all-gather.10
  868.2 55.0 reduce-scatter.3
where the time goes:
time: 933 us; the launch traced here: 931 us
  waiting for transfers between devices  853 us (91%)
  starting transfers between devices  29 us (3%)
  local copies, waits for them, and re-layouts  18.3 us (2%)
  matrix products  15.7 us (2%)
  between operations  13.2 us (1%)
    all_gather x1, waiting for transfers between devices, body(): lax.all_gather(partner[1], 'seq', axis=1, tiled=True)  217 us
    all_gather x1, waiting for transfers between devices, body(): lax.all_gather(key_proj, 'seq', axis=1, tiled=True)  200 us
    all_gather x1, waiting for transfers between devices, body(): lax.all_gather(partner[0], 'seq', axis=1, tiled=True)  192 us
    all_gather x1, waiting for transfers between devices, body(): lax.all_gather(value_proj, 'seq', axis=1, tiled=True)  184 us
    unnamed x6, waiting for transfers between devices  56 us
    ppermute x2, starting transfers between devices, from_behind(): lax.ppermute(value, axis, [(source, source + steps) for source in range(f...  28.8 us
  transfers between devices with their start and end apart: 7, of which 7 were waited for; matrix products, arithmetic and copies ran while one was open for 2% of the time, Pallas kernels for 0%

commit v1 on v0

v1 whole, which is shorter than its diff:
```python
import math

import jax
import jax.numpy as jnp
from jax import lax
from jax.experimental import pallas as pl
from jax.experimental.pallas import tpu as pltpu
from jax.sharding import Mesh, PartitionSpec as P

DH = 128
BLOCK = 128
SCALE_LOG2 = math.log2(math.e) / math.sqrt(DH)
TAIL = 16
KEY_AXES = ("branch", "z2", "z1")
ROW_AXES = ("y", "z0")
HEAD_AXES = ("x", "core")


def attend_kernel(edit_ref, q_ref, k_ref, v_ref, out_ref, wide_ref, tail_ref):
    head = pl.program_id(0)
    heads = pl.num_programs(0)
    row_blocks = out_ref.shape[0]
    key_count = k_ref.shape[0]

    def attend(count):
        keys = k_ref[:count, :]
        wide_ref[:count, :DH] = v_ref[:count, :]
        wide_ref[:count, DH:] = jnp.ones((count, DH), jnp.bfloat16)
        for block in range(row_blocks):
            queries = q_ref[block * BLOCK : (block + 1) * BLOCK, :]
            scores = lax.dot_general(
                queries, keys, (((1,), (1,)), ((), ())), preferred_element_type=jnp.float32
            )
            peak = jnp.max(scores, axis=1, keepdims=True)
            weights = jnp.exp2((scores - peak) * SCALE_LOG2).astype(jnp.bfloat16)
            both = jnp.dot(weights, wide_ref[:count, :], preferred_element_type=jnp.float32)
            total = both[:, DH:]
            out_ref[block, pl.ds(pl.multiple_of(head * BLOCK, BLOCK), BLOCK), :] = (
                both[:, :DH] / total
            ).astype(jnp.bfloat16)
            level = peak * SCALE_LOG2 + jnp.log2(total)
            tail_ref[block, pl.ds(head, 1), :] = level.T[:1, :]

    @pl.when(edit_ref[0] == 1)
    def _():
        attend(key_count)

    @pl.when(edit_ref[0] != 1)
    def _():
        attend(key_count // 2)

    @pl.when(head == heads - 1)
    def _():
        level = tail_ref[:, :4, :]
        high = level.astype(jnp.bfloat16).astype(jnp.float32)
        middle = (level - high).astype(jnp.bfloat16).astype(jnp.float32)
        low = level - high - middle
        pieces = jnp.concatenate([high, middle, low, jnp.zeros_like(low)], axis=1)
        out_ref[:, heads_rows(out_ref) :, :] = pieces.astype(jnp.bfloat16)


def heads_rows(ref):
    return ref.shape[1] - TAIL


def attend(edit, queries, keys_values):
    rows, feats = queries.shape
    keys = keys_values.shape[0]
    heads = feats // DH
    blocks = rows // BLOCK
    return pl.pallas_call(
        attend_kernel,
        grid=(heads,),
        out_shape=jax.ShapeDtypeStruct((blocks, heads * BLOCK + TAIL, DH), jnp.bfloat16),
        in_specs=[
            pl.BlockSpec(memory_space=pltpu.SMEM),
            pl.BlockSpec((rows, DH), lambda h: (0, h)),
            pl.BlockSpec((keys, DH), lambda h: (0, h)),
            pl.BlockSpec((keys, DH), lambda h: (0, heads + h)),
        ],
        out_specs=pl.BlockSpec((blocks, heads * BLOCK + TAIL, DH), lambda h: (0, 0, 0)),
        scratch_shapes=[
            pltpu.VMEM((keys, 2 * DH), jnp.bfloat16),
            pltpu.VMEM((blocks, 8, BLOCK), jnp.float32),
        ],
        compiler_params=pltpu.CompilerParams(vmem_limit_bytes=32 * 1024 * 1024),
        cost_estimate=pl.CostEstimate(
            flops=4 * rows * keys * feats,
            bytes_accessed=2 * (2 * rows * feats + 2 * keys * feats),
            transcendentals=rows * keys * heads,
        ),
    )(edit, queries, keys_values, keys_values)


def merge_kernel(parts_ref, out_ref):
    count, height, _ = parts_ref.shape
    heads = (height - TAIL) // BLOCK
    tail = parts_ref[:, height - TAIL :, :].astype(jnp.float32)
    level = tail[:, :4, :] + tail[:, 4:8, :] + tail[:, 8:12, :]
    share = jnp.exp2(level - jnp.max(level, axis=0, keepdims=True))
    share = share / jnp.sum(share, axis=0, keepdims=True)
    flat = jnp.concatenate(
        [share.reshape(count * 4, BLOCK), jnp.zeros((BLOCK - count * 4, BLOCK), jnp.float32)], axis=0
    )
    turned = flat.T
    for head in range(heads):
        total = jnp.zeros((BLOCK, DH), jnp.float32)
        for part in range(count):
            column = part * 4 + head
            values = parts_ref[part, head * BLOCK : (head + 1) * BLOCK, :].astype(jnp.float32)
            total = total + values * turned[:, column : column + 1]
        out_ref[:, head * DH : (head + 1) * DH] = total.astype(jnp.bfloat16)


def merge(parts):
    heads = (parts.shape[1] - TAIL) // BLOCK
    return pl.pallas_call(
        merge_kernel,
        out_shape=jax.ShapeDtypeStruct((BLOCK, heads * DH), jnp.bfloat16),
        compiler_params=pltpu.CompilerParams(vmem_limit_bytes=16 * 1024 * 1024),
        cost_estimate=pl.CostEstimate(
            flops=2 * parts.size, bytes_accessed=2 * parts.size, transcendentals=0
        ),
    )(parts)


def project_kernel(attended_ref, weight_ref, out_ref):
    count, _, feats = attended_ref.shape
    total = jnp.zeros(out_ref.shape, jnp.float32)
    for part in range(count):
        total = total + jnp.dot(
            attended_ref[part],
            weight_ref[part * feats : (part + 1) * feats, :],
            preferred_element_type=jnp.float32,
        )
    out_ref[...] = total.astype(jnp.bfloat16)


def project(attended, weight):
    count, rows, feats = attended.shape
    columns = weight.shape[1]
    return pl.pallas_call(
        project_kernel,
        out_shape=jax.ShapeDtypeStruct((rows, columns), jnp.bfloat16),
        compiler_params=pltpu.CompilerParams(vmem_limit_bytes=16 * 1024 * 1024),
        cost_estimate=pl.CostEstimate(
            flops=2 * count * rows * feats * columns,
            bytes_accessed=2 * (attended.size + weight.size),
            transcendentals=0,
        ),
    )(attended, weight)


def body(query_proj, key_proj, value_proj, out_weight):
    own = jnp.concatenate([key_proj[0], value_proj[0]], axis=1)
    keys_values = lax.all_gather(own, KEY_AXES, axis=0, tiled=True)
    queries = lax.all_gather(query_proj[0], ROW_AXES, axis=0, tiled=True)
    weight = lax.all_to_all(out_weight, HEAD_AXES, split_axis=1, concat_axis=0, tiled=True)
    keys_values, queries, weight = lax.optimization_barrier((keys_values, queries, weight))
    edit = lax.axis_index("branch").astype(jnp.int32).reshape(1)
    partial = attend(edit, queries, keys_values)
    parts = lax.all_to_all(partial, ROW_AXES, split_axis=0, concat_axis=0, tiled=True)
    attended = merge(parts)
    gathered = lax.all_gather(attended, HEAD_AXES, axis=0, tiled=False)
    return project(gathered, weight)[None]


def solution(mesh):
    split = Mesh(
        mesh.devices.reshape(2, 4, 2, 2, 2, 4, 2),
        ("branch", "y", "z2", "z1", "z0", "x", "core"),
    )
    rows = ("y", "z2", "z1", "z0")
    placed = P("branch", rows, HEAD_AXES)
    return jax.shard_map(
        body,
        mesh=split,
        in_specs=(placed, placed, placed, P(HEAD_AXES, None)),
        out_specs=placed,
        check_vma=False,
    )
```

time: 933 us -> 125 us (0.13)
  waiting for transfers between devices: 853 us -> 20.2 us
  blocking collectives: 0 us -> 68.8 us
  starting transfers between devices: 29 us -> 10.5 us
  matrix products: 15.7 us -> 0 us
  local copies, waits for them, and re-layouts: 18.3 us -> 4.74 us
    all_gather x4 -> x1, waiting for transfers between devices: 793 us -> 20.2 us  [body(): keys_values = lax.all_gather(own, KEY_AXES, axis=0, tiled=True)]
    unnamed x6 -> x1, waiting for transfers between devices: 56 us -> 0.02 us
    all_gather x0 -> x2, blocking collectives: none -> 55.3 us  [the longest x1 38.2 us: body(): queries = lax.all_gather(query_proj[0], ROW_AXES, axis=0, tiled=True)]
    ppermute x2 -> x0, starting transfers between devices: 28.8 us -> none  [from_behind(): lax.ppermute(value, axis, [(source, source + steps) for source in range(f...]
    dot_general x5 -> x0, matrix products: 15.7 us -> none  [the longest x2 8.82 us: attend_piece(): jnp.einsum('rhd,nhd->hrn', query_heads, key_heads, preferred_element_type...]
    all_to_all x0 -> x1, blocking collectives: none -> 13.5 us  [body(): lax.all_to_all(partial, ROW_AXES, split_axis=0, concat_axis=0, tiled=True)]
    all_to_all x0 -> x1, starting transfers between devices: none -> 10.5 us  [body(): lax.all_to_all(out_weight, HEAD_AXES, split_axis=1, concat_axis=0, tiled=...]
    all_gather x2 -> x0, local copies, waits for them, and re-layouts: 9.43 us -> none  [the longest x1 4.78 us: body(): lax.all_gather(partner[1], 'seq', axis=1, tiled=True)]
  transfers between devices with their start and end apart: 7 -> 2, of which waited for: 7 -> 1; matrix products, arithmetic and copies ran while one was open for 2% -> 3% of each run, Pallas kernels for 0% -> 0%
where the time goes in v1:
time: 125 us
  blocking collectives  68.8 us (55%)
  waiting for transfers between devices  20.2 us (16%)
  between operations  13.4 us (11%)
  starting transfers between devices  10.5 us (8%)
  Pallas kernels  5.46 us (4%)
  local copies, waits for them, and re-layouts  4.74 us (4%)
  other arithmetic  1.63 us (1%)
    all_gather x1, blocking collectives, body(): queries = lax.all_gather(query_proj[0], ROW_AXES, axis=0, tiled=True)  38.2 us
    all_gather x1, waiting for transfers between devices, body(): keys_values = lax.all_gather(own, KEY_AXES, axis=0, tiled=True)  20.2 us
    all_gather x1, blocking collectives, body(): gathered = lax.all_gather(attended, HEAD_AXES, axis=0, tiled=False)  17.1 us
    all_to_all x1, blocking collectives, body(): lax.all_to_all(partial, ROW_AXES, split_axis=0, concat_axis=0, tiled=True)  13.5 us
    all_to_all x1, starting transfers between devices, body(): lax.all_to_all(out_weight, HEAD_AXES, split_axis=1, concat_axis=0, tiled=...  10.5 us
    pallas_call x1, Pallas kernels, attend(): pl.pallas_call(attend_kernel, grid=(heads,), out_shape=jax.ShapeDtypeStru...  3.52 us
    all_to_all x1, local copies, waits for them, and re-layouts, body(): lax.all_to_all(out_weight, HEAD_AXES, split_axis=1, concat_axis=0, tiled=...  3.33 us
  transfers between devices with their start and end apart: 2, of which 1 were waited for; matrix products, arithmetic and copies ran while one was open for 3% of the time, Pallas kernels for 0%

profile of v1, /device:TPU:1, one launch (start us, length us, event | category | flops | bytes accessed | tf_op | source)
XLA Modules:
  0.0 124.8 jit_solution(491641518188444644)
XLA Ops:
  6.5 0.0 all-gather.4.cloned.1.call-start
  6.5 1.6 %pad_maximum_fusion = bf16[128,768]{1,0:T(8,128)(2,1)} fusion(bf16[128,384]{1,0:T(8,128)(2,1)} %bitcast.18, bf16[128,384]{1,0:T(8,128)(2,1)} %bitcast.19), kind=kLoop, calls=%fused_computation.1 | loop fusion | flops 393216 | bytes 393216 | tf_op jit(solution)/shard_map/concatenate | solution.py:155
  8.2 0.0 all-gather.4.cloned.1.call-update
  8.2 3.3 %copy.8 = bf16[48,8,8,384]{3,2,0,1:T(8,128)(2,1)} copy(bf16[48,8,8,384]{3,2,1,0:T(8,128)(2,1)} %bitcast.17) | data formatting | bytes 4718592 | tf_op jit(solution)/shard_map/all_to_all | solution.py:158
  11.5 0.0 copy-start.1
  11.5 10.5 %all-to-all-start = ((bf16[384,8,384]{2,0,1:T(8,128)(2,1)}), bf16[384,8,384]{2,0,1:T(8,128)(2,1)S(1)}, u32[]{:S(2)}, u32[]{:S(2)}) async-start(bf16[384,8,384]{2,0,1:T(8,128)(2,1)} %bitcast.16), calls=%async_computation | async-start | bytes 4718592 | tf_op jit(solution)/shard_map/all_to_all | solution.py:158
  22.1 0.0 copy-done.1
  22.1 38.2 %all-gather = bf16[1,1024,384]{2,1,0:T(8,128)(2,1)S(1)} all-gather(bf16[1,128,384]{2,1,0:T(8,128)(2,1)S(1)} %copy-done.1), channel_id=2, replica_groups=mesh['branch'=2,'y'=4,'z2'=2,'z1'=2,'z0'=2,'x'=4,'core'=2] {'y','z0'}, dimensions={1}, use_global_device_ids=true | all-gather | bytes 884736 | tf_op jit(solution)/shard_map/all_gather | solution.py:157
  60.3 0.0 all-to-all-done
  60.3 20.2 %all-gather.4.cloned.1.call-done.k_ref.v_ref = bf16[1024,768]{1,0:T(8,128)(2,1)} async-done(((bf16[128,768]{1,0:T(8,128)(2,1)}), bf16[1024,768]{1,0:T(8,128)(2,1)}) %all-gather.4.cloned.1.call-update) | async-done | bytes 1572880 | tf_op jit(solution)/shard_map/all_gather | solution.py:156
  80.5 0.0 copy-start
  80.5 1.4 %copy-done = bf16[1024,768]{1,0:T(8,128)(2,1)S(1)} copy-done((bf16[1024,768]{1,0:T(8,128)(2,1)S(1)}, bf16[1024,768]{1,0:T(8,128)(2,1)}, u32[]{:S(2)}) %copy-start) | copy-done | bytes 1572888
  81.9 3.5 %shard_map.46 = bf16[8,400,128]{2,1,0:T(8,128)(2,1)S(1)} custom-call(s32[1]{0:T(128)} %bitcast.edit_ref, bf16[1024,384]{1,0:T(8,128)(2,1)S(1)} %bitcast.15, bf16[1024,768]{1,0:T(8,128)(2,1)S(1)} %copy-done, bf16[1024,768]{1,0:T(8,128)(2,1)S(1)} %copy-done), custom_call_target="tpu_custom_call" | custom-call | flops 1610612736 | bytes 3145728 | tf_op jit(solution)/shard_map/pallas_call | solution.py:71
  85.4 13.5 %all_to_all.24.parts_ref = bf16[8,400,128]{2,1,0:T(8,128)(2,1)S(1)} all-to-all(bf16[8,400,128]{2,1,0:T(8,128)(2,1)S(1)} %shard_map.46), channel_id=1, replica_groups=mesh['branch'=2,'y'=4,'z2'=2,'z1'=2,'z0'=2,'x'=4,'core'=2] {'y','z0'}, dimensions={0} | all-to-all | bytes 1638400 | tf_op jit(solution)/shard_map/all_to_all | solution.py:162
  98.9 0.7 shard_map.47
  99.6 17.1 %all-gather.1 = bf16[1024,384]{1,0:T(8,128)(2,1)S(1)} all-gather(bf16[128,384]{1,0:T(8,128)(2,1)S(1)} %shard_map.47), channel_id=3, replica_groups=mesh['branch'=2,'y'=4,'z2'=2,'z1'=2,'z0'=2,'x'=4,'core'=2] {'x','core'}, dimensions={0}, use_global_device_ids=true | all-gather | bytes 884736 | tf_op jit(solution)/shard_map/all_gather | solution.py:164
  116.7 1.3 %shard_map.48 = bf16[128,384]{1,0:T(8,128)(2,1)} custom-call(bf16[8,128,384]{2,1,0:T(8,128)(2,1)S(1)} %bitcast.14, bf16[3072,384]{1,0:T(8,128)(2,1)S(1)} %bitcast.13), custom_call_target="tpu_custom_call" | custom-call | flops 301989888 | bytes 3145728 | tf_op jit(solution)/shard_map/pallas_call | solution.py:142
Async XLA Ops:
  6.5 73.9 %all-gather.4.cloned.1.call-start = ((), (), s32[]{:S(2)}) async-start(), calls=%async_computation.2 | async-start | bytes 1769472 | tf_op jit(solution)/shard_map/all_gather | solution.py:156
  11.5 10.5 %copy-start.1 = (bf16[1,128,384]{2,1,0:T(8,128)(2,1)S(1)}, bf16[1,128,384]{2,1,0:T(8,128)(2,1)}, u32[]{:S(2)}) copy-start(bf16[1,128,384]{2,1,0:T(8,128)(2,1)} %param.4) | copy-start | bytes 294916
  11.5 48.8 %all-to-all-start = ((bf16[384,8,384]{2,0,1:T(8,128)(2,1)}), bf16[384,8,384]{2,0,1:T(8,128)(2,1)S(1)}, u32[]{:S(2)}, u32[]{:S(2)}) async-start(bf16[384,8,384]{2,0,1:T(8,128)(2,1)} %bitcast.16), calls=%async_computation | async-start | bytes 4718592 | tf_op jit(solution)/shard_map/all_to_all | solution.py:158
  80.5 1.4 %copy-start = (bf16[1024,768]{1,0:T(8,128)(2,1)S(1)}, bf16[1024,768]{1,0:T(8,128)(2,1)}, u32[]{:S(2)}) copy-start(bf16[1024,768]{1,0:T(8,128)(2,1)} %all-gather.4.cloned.1.call-done.k_ref.v_ref) | copy-start | bytes 4718596
Sparse Core Ops, SparseCore 0:
  9.4 71.0 all-gather.3

commit v2 on v1

--- a/solution.py
+++ b/solution.py
@@ -16,7 +16,7 @@
 HEAD_AXES = ("x", "core")
 
 
-def attend_kernel(edit_ref, q_ref, k_ref, v_ref, out_ref, wide_ref, tail_ref):
+def attend_kernel(place_ref, q_ref, k_ref, v_ref, out_ref, wide_ref, tail_ref):
     head = pl.program_id(0)
     heads = pl.num_programs(0)
     row_blocks = out_ref.shape[0]
@@ -27,6 +27,7 @@
         wide_ref[:count, :DH] = v_ref[:count, :]
         wide_ref[:count, DH:] = jnp.ones((count, DH), jnp.bfloat16)
         for block in range(row_blocks):
+            target = block // 2 * 2 + (block % 2 ^ place_ref[1])
             queries = q_ref[block * BLOCK : (block + 1) * BLOCK, :]
             scores = lax.dot_general(
                 queries, keys, (((1,), (1,)), ((), ())), preferred_element_type=jnp.float32
@@ -35,17 +36,17 @@
             weights = jnp.exp2((scores - peak) * SCALE_LOG2).astype(jnp.bfloat16)
             both = jnp.dot(weights, wide_ref[:count, :], preferred_element_type=jnp.float32)
             total = both[:, DH:]
-            out_ref[block, pl.ds(pl.multiple_of(head * BLOCK, BLOCK), BLOCK), :] = (
+            out_ref[target, pl.ds(pl.multiple_of(head * BLOCK, BLOCK), BLOCK), :] = (
                 both[:, :DH] / total
             ).astype(jnp.bfloat16)
             level = peak * SCALE_LOG2 + jnp.log2(total)
-            tail_ref[block, pl.ds(head, 1), :] = level.T[:1, :]
+            tail_ref[target, pl.ds(head, 1), :] = level.T[:1, :]
 
-    @pl.when(edit_ref[0] == 1)
+    @pl.when(place_ref[0] == 1)
     def _():
         attend(key_count)
 
-    @pl.when(edit_ref[0] != 1)
+    @pl.when(place_ref[0] != 1)
     def _():
         attend(key_count // 2)
 
@@ -63,7 +64,7 @@
     return ref.shape[1] - TAIL
 
 
-def attend(edit, queries, keys_values):
+def attend(place, queries, keys_values):
     rows, feats = queries.shape
     keys = keys_values.shape[0]
     heads = feats // DH
@@ -83,13 +84,13 @@
             pltpu.VMEM((keys, 2 * DH), jnp.bfloat16),
             pltpu.VMEM((blocks, 8, BLOCK), jnp.float32),
         ],
-        compiler_params=pltpu.CompilerParams(vmem_limit_bytes=32 * 1024 * 1024),
+        compiler_params=pltpu.CompilerParams(vmem_limit_bytes=60 * 1024 * 1024),
         cost_estimate=pl.CostEstimate(
             flops=4 * rows * keys * feats,
             bytes_accessed=2 * (2 * rows * feats + 2 * keys * feats),
             transcendentals=rows * keys * heads,
         ),
-    )(edit, queries, keys_values, keys_values)
+    )(place, queries, keys_values, keys_values)
 
 
 def merge_kernel(parts_ref, out_ref):
@@ -154,11 +155,13 @@
 def body(query_proj, key_proj, value_proj, out_weight):
     own = jnp.concatenate([key_proj[0], value_proj[0]], axis=1)
     keys_values = lax.all_gather(own, KEY_AXES, axis=0, tiled=True)
-    queries = lax.all_gather(query_proj[0], ROW_AXES, axis=0, tiled=True)
+    beside = lax.ppermute(query_proj[0], "z0", [(0, 1), (1, 0)])
+    queries = jnp.concatenate([query_proj[0], beside], axis=0)
+    queries = lax.all_gather(queries, "y", axis=0, tiled=True)
     weight = lax.all_to_all(out_weight, HEAD_AXES, split_axis=1, concat_axis=0, tiled=True)
     keys_values, queries, weight = lax.optimization_barrier((keys_values, queries, weight))
-    edit = lax.axis_index("branch").astype(jnp.int32).reshape(1)
-    partial = attend(edit, queries, keys_values)
+    place = jnp.stack([lax.axis_index("branch"), lax.axis_index("z0")]).astype(jnp.int32)
+    partial = attend(place, queries, keys_values)
     parts = lax.all_to_all(partial, ROW_AXES, split_axis=0, concat_axis=0, tiled=True)
     attended = merge(parts)
     gathered = lax.all_gather(attended, HEAD_AXES, axis=0, tiled=False)

time: 125 us -> 119 us (0.952)
  blocking collectives: 68.8 us -> 45.4 us
  waiting for transfers between devices: 20.2 us -> 34.4 us
  starting transfers between devices: 10.5 us -> 12.4 us
  Pallas kernels: 5.46 us -> 7.15 us
  local copies, waits for them, and re-layouts: 4.74 us -> 3.34 us
    all_gather x1, blocking collectives: 38.2 us -> 11.6 us  [body(): queries = lax.all_gather(queries, 'y', axis=0, tiled=True)]
    all_to_all x1, waiting for transfers between devices: 0.01 us -> 11.4 us  [body(): lax.all_to_all(out_weight, HEAD_AXES, split_axis=1, concat_axis=0, tiled=...]
    ppermute x0 -> x1, waiting for transfers between devices: none -> 3.64 us  [body(): beside = lax.ppermute(query_proj[0], 'z0', [(0, 1), (1, 0)])]
    all_to_all x1, blocking collectives: 13.5 us -> 17.1 us  [body(): lax.all_to_all(partial, ROW_AXES, split_axis=0, concat_axis=0, tiled=True)]
    ppermute x0 -> x1, starting transfers between devices: none -> 1.91 us  [body(): beside = lax.ppermute(query_proj[0], 'z0', [(0, 1), (1, 0)])]
    pallas_call x1, Pallas kernels: 3.52 us -> 5.2 us  [attend(): pl.pallas_call(attend_kernel, grid=(heads,), out_shape=jax.ShapeDtypeStru...]
    unnamed x4 -> x2, local copies, waits for them, and re-layouts: 1.41 us -> 0.01 us
  transfers between devices with their start and end apart: 2 -> 3, of which waited for: 1 -> 3; matrix products, arithmetic and copies ran while one was open for 3% -> 3% of each run, Pallas kernels for 0% -> 0%
where the time goes in v2:
time: 119 us; the launch traced here: 118 us
  blocking collectives  45.4 us (38%)
  waiting for transfers between devices  34.4 us (29%)
  between operations  13.4 us (11%)
  starting transfers between devices  12.4 us (10%)
  Pallas kernels  7.15 us (6%)
  local copies, waits for them, and re-layouts  3.34 us (3%)
  other arithmetic  2.23 us (2%)
    all_gather x1, waiting for transfers between devices, body(): keys_values = lax.all_gather(own, KEY_AXES, axis=0, tiled=True)  19.3 us
    all_to_all x1, blocking collectives, body(): lax.all_to_all(partial, ROW_AXES, split_axis=0, concat_axis=0, tiled=True)  17.1 us
    all_gather x1, blocking collectives, body(): gathered = lax.all_gather(attended, HEAD_AXES, axis=0, tiled=False)  16.8 us
    all_gather x1, blocking collectives, body(): queries = lax.all_gather(queries, 'y', axis=0, tiled=True)  11.6 us
    all_to_all x1, waiting for transfers between devices, body(): lax.all_to_all(out_weight, HEAD_AXES, split_axis=1, concat_axis=0, tiled=...  11.4 us
    all_to_all x1, starting transfers between devices, body(): lax.all_to_all(out_weight, HEAD_AXES, split_axis=1, concat_axis=0, tiled=...  10.5 us
    pallas_call x1, Pallas kernels, attend(): pl.pallas_call(attend_kernel, grid=(heads,), out_shape=jax.ShapeDtypeStru...  5.2 us
    ppermute x1, waiting for transfers between devices, body(): beside = lax.ppermute(query_proj[0], 'z0', [(0, 1), (1, 0)])  3.64 us
  transfers between devices with their start and end apart: 3, of which 3 were waited for; matrix products, arithmetic and copies ran while one was open for 3% of the time, Pallas kernels for 0%

profile of v2, /device:TPU:1, one launch (start us, length us, event | category | flops | bytes accessed | tf_op | source)
XLA Modules:
  0.0 118.4 jit_solution(11528475739989823302)
XLA Ops:
  6.5 0.0 all-gather.3.cloned.1.call-start
  6.5 1.6 %pad_maximum_fusion = bf16[128,768]{1,0:T(8,128)(2,1)} fusion(bf16[128,384]{1,0:T(8,128)(2,1)} %bitcast.18, bf16[128,384]{1,0:T(8,128)(2,1)} %bitcast.19), kind=kLoop, calls=%fused_computation.1 | loop fusion | flops 393216 | bytes 393216 | tf_op jit(solution)/shard_map/concatenate | solution.py:156
  8.2 0.0 all-gather.3.cloned.1.call-update
  8.2 3.3 %copy.8 = bf16[48,8,8,384]{3,2,0,1:T(8,128)(2,1)} copy(bf16[48,8,8,384]{3,2,1,0:T(8,128)(2,1)} %bitcast.17) | data formatting | bytes 4718592 | tf_op jit(solution)/shard_map/all_to_all | solution.py:161
  11.5 0.0 copy-start
  11.5 10.5 %all-to-all-start = ((bf16[384,8,384]{2,0,1:T(8,128)(2,1)}), bf16[384,8,384]{2,0,1:T(8,128)(2,1)S(1)}, u32[]{:S(2)}, u32[]{:S(2)}) async-start(bf16[384,8,384]{2,0,1:T(8,128)(2,1)} %bitcast.16), calls=%async_computation | async-start | bytes 4718592 | tf_op jit(solution)/shard_map/all_to_all | solution.py:161
  22.1 0.0 copy-done
  22.1 1.9 %collective-permute-start = (bf16[128,384]{1,0:T(8,128)(2,1)S(1)}, bf16[128,384]{1,0:T(8,128)(2,1)S(1)}, u32[]{:S(2)}, u32[]{:S(2)}) collective-permute-start(bf16[128,384]{1,0:T(8,128)(2,1)S(1)} %bitcast.20), channel_id=1, source_target_pairs={{0,8},{8,0},{1,9},{9,1},{2,10},{10,2},{3,11},{11,3},{4,12},{12,4},... | collective-permute-start | bytes 294920 | tf_op jit(solution)/shard_map/ppermute | solution.py:158
  24.0 0.6 pad_add_fusion.place_ref
  24.6 3.6 %collective-permute-done = bf16[128,384]{1,0:T(8,128)(2,1)S(1)} collective-permute-done((bf16[128,384]{1,0:T(8,128)(2,1)S(1)}, bf16[128,384]{1,0:T(8,128)(2,1)S(1)}, u32[]{:S(2)}, u32[]{:S(2)}) %collective-permute-start) | collective-permute-done | bytes 98336 | tf_op jit(solution)/shard_map/ppermute | solution.py:158
  28.2 11.6 %all_gather.13.q_ref = bf16[1024,384]{1,0:T(8,128)(2,1)} all-gather(bf16[256,384]{1,0:T(8,128)(2,1)S(1)} %pad_maximum_fusion.1), channel_id=1, replica_groups=mesh['branch'=2,'y'=4,'z2'=2,'z1'=2,'z0'=2,'x'=4,'core'=2] {'y'}, dimensions={0}, use_global_device_ids=true | all-gather | bytes 983040 | tf_op jit(solution)/shard_map/all_gather | solution.py:160
  39.8 11.4 %all-to-all-done = bf16[384,8,384]{2,0,1:T(8,128)(2,1)S(1)} async-done(((bf16[384,8,384]{2,0,1:T(8,128)(2,1)}), bf16[384,8,384]{2,0,1:T(8,128)(2,1)S(1)}, u32[]{:S(2)}, u32[]{:S(2)}) %all-to-all-start) | async-done | bytes 2359328 | tf_op jit(solution)/shard_map/all_to_all | solution.py:161
  51.2 19.3 %all-gather.3.cloned.1.call-done.k_ref.v_ref = bf16[1024,768]{1,0:T(8,128)(2,1)} async-done(((bf16[128,768]{1,0:T(8,128)(2,1)}), bf16[1024,768]{1,0:T(8,128)(2,1)}) %all-gather.3.cloned.1.call-update) | async-done | bytes 1572880 | tf_op jit(solution)/shard_map/all_gather | solution.py:157
  70.5 5.2 %shard_map.46 = bf16[8,400,128]{2,1,0:T(8,128)(2,1)} custom-call(s32[2]{0:T(128)} %pad_add_fusion.place_ref, bf16[1024,384]{1,0:T(8,128)(2,1)} %all_gather.13.q_ref, bf16[1024,768]{1,0:T(8,128)(2,1)} %all-gather.3.cloned.1.call-done.k_ref.v_ref, bf16[1024,768]{1,0:T(8,128)(2,1)} %all-gather.3.cloned.1.call-done.k_ref.v_ref), custom_call_target="tpu_custom_call" | custom-call | flops 1610612736 | bytes 3145728 | tf_op jit(solution)/shard_map/pallas_call | solution.py:72
  75.7 17.1 %all_to_all.24.parts_ref = bf16[8,400,128]{2,1,0:T(8,128)(2,1)S(1)} all-to-all(bf16[8,400,128]{2,1,0:T(8,128)(2,1)} %shard_map.46), channel_id=1, replica_groups=mesh['branch'=2,'y'=4,'z2'=2,'z1'=2,'z0'=2,'x'=4,'core'=2] {'y','z0'}, dimensions={0} | all-to-all | bytes 1638400 | tf_op jit(solution)/shard_map/all_to_all | solution.py:165
  92.8 0.7 shard_map.47
  93.5 16.8 %all-gather = bf16[1024,384]{1,0:T(8,128)(2,1)S(1)} all-gather(bf16[128,384]{1,0:T(8,128)(2,1)S(1)} %shard_map.47), channel_id=2, replica_groups=mesh['branch'=2,'y'=4,'z2'=2,'z1'=2,'z0'=2,'x'=4,'core'=2] {'x','core'}, dimensions={0}, use_global_device_ids=true | all-gather | bytes 884736 | tf_op jit(solution)/shard_map/all_gather | solution.py:167
  110.3 1.3 %shard_map.48 = bf16[128,384]{1,0:T(8,128)(2,1)} custom-call(bf16[8,128,384]{2,1,0:T(8,128)(2,1)S(1)} %bitcast.15, bf16[3072,384]{1,0:T(8,128)(2,1)S(1)} %bitcast.14), custom_call_target="tpu_custom_call" | custom-call | flops 301989888 | bytes 3145728 | tf_op jit(solution)/shard_map/pallas_call | solution.py:143
  (1 shorter events, 0.0 us)
Async XLA Ops:
  6.5 64.0 %all-gather.3.cloned.1.call-start = ((), (), s32[]{:S(2)}) async-start(), calls=%async_computation.2 | async-start | bytes 1769472 | tf_op jit(solution)/shard_map/all_gather | solution.py:157
  11.5 10.5 %copy-start = (bf16[1,128,384]{2,1,0:T(8,128)(2,1)S(1)}, bf16[1,128,384]{2,1,0:T(8,128)(2,1)}, u32[]{:S(2)}) copy-start(bf16[1,128,384]{2,1,0:T(8,128)(2,1)} %param.4) | copy-start | bytes 294916
  11.5 39.7 %all-to-all-start = ((bf16[384,8,384]{2,0,1:T(8,128)(2,1)}), bf16[384,8,384]{2,0,1:T(8,128)(2,1)S(1)}, u32[]{:S(2)}, u32[]{:S(2)}) async-start(bf16[384,8,384]{2,0,1:T(8,128)(2,1)} %bitcast.16), calls=%async_computation | async-start | bytes 4718592 | tf_op jit(solution)/shard_map/all_to_all | solution.py:161
  22.1 6.1 %collective-permute-start = (bf16[128,384]{1,0:T(8,128)(2,1)S(1)}, bf16[128,384]{1,0:T(8,128)(2,1)S(1)}, u32[]{:S(2)}, u32[]{:S(2)}) collective-permute-start(bf16[128,384]{1,0:T(8,128)(2,1)S(1)} %bitcast.20), channel_id=1, source_target_pairs={{0,8},{8,0},{1,9},{9,1},{2,10},{10,2},{3,11},{11,3},{4,12},{12,4},... | collective-permute-start | bytes 294920 | tf_op jit(solution)/shard_map/ppermute | solution.py:158
Sparse Core Ops, SparseCore 0:
  9.4 61.0 all-gather.2

commit v3 on v1

v3 whole, which is shorter than its diff:
```python
import math

import jax
import jax.numpy as jnp
from jax import lax
from jax.experimental import pallas as pl
from jax.experimental.pallas import tpu as pltpu
from jax.sharding import Mesh, PartitionSpec as P

DH = 128
BLOCK = 128
KEY_SHIFT = 13
SCALE_LOG2 = math.log2(math.e) / math.sqrt(DH) / 2.0**KEY_SHIFT
TAIL = 16
KEY_AXES = ("branch", "z2", "z1")
ROW_AXES = ("y", "z0")
HEAD_AXES = ("x", "core")


def pack_kernel(key_ref, value_ref, out_ref):
    feats = key_ref.shape[1]
    out_ref[:, :feats] = (key_ref[...].astype(jnp.float32) * 2.0**KEY_SHIFT).astype(jnp.bfloat16)
    values = value_ref[...].astype(jnp.float32)
    largest = jnp.max(jnp.abs(values), axis=1, keepdims=True)
    power = jnp.floor(jnp.log2(jnp.maximum(largest, 2.0**-100)))
    power = jnp.broadcast_to(power, (values.shape[0], DH))
    factor = jnp.exp2(14.0 - power)
    for head in range(feats // DH):
        part = values[:, head * DH : (head + 1) * DH]
        out_ref[:, feats + head * DH : feats + (head + 1) * DH] = (part * factor).astype(jnp.bfloat16)
    out_ref[:, 2 * feats :] = power.astype(jnp.bfloat16)


def pack(keys, values):
    rows, feats = keys.shape
    return pl.pallas_call(
        pack_kernel,
        out_shape=jax.ShapeDtypeStruct((rows, 2 * feats + DH), jnp.bfloat16),
        cost_estimate=pl.CostEstimate(
            flops=4 * rows * feats, bytes_accessed=8 * rows * feats, transcendentals=2 * rows * DH
        ),
    )(keys, values)


def attend_kernel(edit_ref, q_ref, k_ref, v_ref, power_ref, out_ref, wide_ref, tail_ref):
    head = pl.program_id(0)
    heads = pl.num_programs(0)
    row_blocks = out_ref.shape[0]
    key_count = k_ref.shape[0]

    def attend(count):
        keys = k_ref[:count, :]
        factor = jnp.exp2(power_ref[:count, :].astype(jnp.float32) - 14.0)
        wide_ref[:count, :DH] = (v_ref[:count, :].astype(jnp.float32) * factor).astype(jnp.bfloat16)
        wide_ref[:count, DH:] = jnp.ones((count, DH), jnp.bfloat16)
        for block in range(row_blocks):
            queries = q_ref[block * BLOCK : (block + 1) * BLOCK, :]
            scores = lax.dot_general(
                queries, keys, (((1,), (1,)), ((), ())), preferred_element_type=jnp.float32
            )
            peak = jnp.max(scores, axis=1, keepdims=True)
            weights = jnp.exp2((scores - peak) * SCALE_LOG2).astype(jnp.bfloat16)
            both = jnp.dot(weights, wide_ref[:count, :], preferred_element_type=jnp.float32)
            total = both[:, DH:]
            out_ref[block, pl.ds(pl.multiple_of(head * BLOCK, BLOCK), BLOCK), :] = (
                both[:, :DH] / total
            ).astype(jnp.bfloat16)
            level = peak * SCALE_LOG2 + jnp.log2(total)
            tail_ref[block, pl.ds(head, 1), :] = level.T[:1, :]

    @pl.when(edit_ref[0] == 1)
    def _():
        attend(key_count)

    @pl.when(edit_ref[0] != 1)
    def _():
        attend(key_count // 2)

    @pl.when(head == heads - 1)
    def _():
        level = tail_ref[:, :4, :]
        high = level.astype(jnp.bfloat16).astype(jnp.float32)
        middle = (level - high).astype(jnp.bfloat16).astype(jnp.float32)
        low = level - high - middle
        pieces = jnp.concatenate([high, middle, low, jnp.zeros_like(low)], axis=1)
        out_ref[:, out_ref.shape[1] - TAIL :, :] = pieces.astype(jnp.bfloat16)


def attend(edit, queries, packed):
    rows, feats = queries.shape
    keys = packed.shape[0]
    heads = feats // DH
    blocks = rows // BLOCK
    return pl.pallas_call(
        attend_kernel,
        grid=(heads,),
        out_shape=jax.ShapeDtypeStruct((blocks, heads * BLOCK + TAIL, DH), jnp.bfloat16),
        in_specs=[
            pl.BlockSpec(memory_space=pltpu.SMEM),
            pl.BlockSpec((rows, DH), lambda h: (0, h)),
            pl.BlockSpec((keys, DH), lambda h: (0, h)),
            pl.BlockSpec((keys, DH), lambda h: (0, heads + h)),
            pl.BlockSpec((keys, DH), lambda h: (0, 2 * heads)),
        ],
        out_specs=pl.BlockSpec((blocks, heads * BLOCK + TAIL, DH), lambda h: (0, 0, 0)),
        scratch_shapes=[
            pltpu.VMEM((keys, 2 * DH), jnp.bfloat16),
            pltpu.VMEM((blocks, 8, BLOCK), jnp.float32),
        ],
        compiler_params=pltpu.CompilerParams(vmem_limit_bytes=32 * 1024 * 1024),
        cost_estimate=pl.CostEstimate(
            flops=4 * rows * keys * feats,
            bytes_accessed=2 * (2 * rows * feats + 2 * keys * feats),
            transcendentals=rows * keys * heads,
        ),
    )(edit, queries, packed, packed, packed)


def merge_kernel(parts_ref, weight_ref, out_ref):
    count, height, _ = parts_ref.shape
    heads = (height - TAIL) // BLOCK
    columns = out_ref.shape[2]
    tail = parts_ref[:, height - TAIL :, :].astype(jnp.float32)
    level = tail[:, :4, :] + tail[:, 4:8, :] + tail[:, 8:12, :]
    share = jnp.exp2(level - jnp.max(level, axis=0, keepdims=True))
    share = share / jnp.sum(share, axis=0, keepdims=True)
    flat = jnp.concatenate(
        [share.reshape(count * 4, BLOCK), jnp.zeros((BLOCK - count * 4, BLOCK), jnp.float32)], axis=0
    )
    turned = flat.T
    merged = []
    for head in range(heads):
        total = jnp.zeros((BLOCK, DH), jnp.float32)
        for part in range(count):
            column = part * 4 + head
            values = parts_ref[part, head * BLOCK : (head + 1) * BLOCK, :].astype(jnp.float32)
            total = total + values * turned[:, column : column + 1]
        merged.append(total.astype(jnp.bfloat16))
    attended = jnp.concatenate(merged, axis=1)
    for target in range(out_ref.shape[0]):
        out_ref[target] = jnp.dot(
            attended,
            weight_ref[:, target * columns : (target + 1) * columns],
            preferred_element_type=jnp.float32,
        ).astype(jnp.bfloat16)


def merge(parts, weight, targets):
    columns = weight.shape[1] // targets
    return pl.pallas_call(
        merge_kernel,
        out_shape=jax.ShapeDtypeStruct((targets, BLOCK, columns), jnp.bfloat16),
        compiler_params=pltpu.CompilerParams(vmem_limit_bytes=16 * 1024 * 1024),
        cost_estimate=pl.CostEstimate(
            flops=2 * BLOCK * weight.size,
            bytes_accessed=2 * (parts.size + weight.size),
            transcendentals=0,
        ),
    )(parts, weight)


def add_kernel(parts_ref, out_ref):
    total = parts_ref[0].astype(jnp.float32)
    for part in range(1, parts_ref.shape[0]):
        total = total + parts_ref[part].astype(jnp.float32)
    out_ref[...] = total.astype(jnp.bfloat16)


def add(parts):
    return pl.pallas_call(
        add_kernel, out_shape=jax.ShapeDtypeStruct(parts.shape[1:], jnp.bfloat16)
    )(parts)


def spread(value, axes):
    count = lax.axis_size(axes)
    copies = jnp.broadcast_to(value[None], (count,) + value.shape)
    return lax.all_to_all(copies, axes, split_axis=0, concat_axis=0, tiled=True)


def body(query_proj, key_proj, value_proj, out_weight):
    queries = spread(query_proj[0], ROW_AXES).reshape(-1, query_proj.shape[2])
    packed = pack(key_proj[0], value_proj[0]).astype(jnp.float16)
    packed = lax.all_gather(packed, KEY_AXES, axis=0, tiled=True).astype(jnp.bfloat16)
    edit = lax.axis_index("branch").astype(jnp.int32).reshape(1)
    partial = attend(edit, queries, packed)
    parts = lax.all_to_all(partial, ROW_AXES, split_axis=0, concat_axis=0, tiled=True)
    shares = merge(parts, out_weight, lax.axis_size(HEAD_AXES))
    shares = lax.all_to_all(shares, HEAD_AXES, split_axis=0, concat_axis=0, tiled=True)
    return add(shares)[None]


def solution(mesh):
    split = Mesh(
        mesh.devices.reshape(2, 4, 2, 2, 2, 4, 2),
        ("branch", "y", "z2", "z1", "z0", "x", "core"),
    )
    rows = ("y", "z2", "z1", "z0")
    placed = P("branch", rows, HEAD_AXES)
    return jax.shard_map(
        body,
        mesh=split,
        in_specs=(placed, placed, placed, P(HEAD_AXES, None)),
        out_specs=placed,
        check_vma=False,
    )
```

time: 125 us -> 105 us (0.84)
  waiting for transfers between devices: 20.2 us -> 0.01 us
  blocking collectives: 68.8 us -> 86.5 us
  between operations: 13.4 us -> 0.05 us
  starting transfers between devices: 10.5 us -> 6.37 us
  Pallas kernels: 5.46 us -> 8.66 us
  local copies, waits for them, and re-layouts: 4.74 us -> 1.86 us
    all_to_all x0 -> x1, blocking collectives: none -> 22.6 us  [body(): lax.all_to_all(shares, HEAD_AXES, split_axis=0, concat_axis=0, tiled=True)]
    all_gather x1 -> x0, waiting for transfers between devices: 20.2 us -> none  [body(): keys_values = lax.all_gather(own, KEY_AXES, axis=0, tiled=True)]
    all_gather x2 -> x1, blocking collectives: 55.3 us -> 49 us  [body(): lax.all_gather(packed, KEY_AXES, axis=0, tiled=True).astype(jnp.bfloat16)]
    all_to_all x1, starting transfers between devices: 10.5 us -> 6.37 us  [spread(): return lax.all_to_all(copies, axes, split_axis=0, concat_axis=0, tiled=True)]
    all_to_all x1 -> x0, local copies, waits for them, and re-layouts: 3.33 us -> none  [body(): lax.all_to_all(out_weight, HEAD_AXES, split_axis=1, concat_axis=0, tiled=...]
    pallas_call x2 -> x3, Pallas kernels: 1.95 us -> 5.06 us  [the longest x1 1.88 us: add(): pl.pallas_call(add_kernel, out_shape=jax.ShapeDtypeStruct(parts.shape[1:]...]
    broadcast_in_dim x0 -> x1, local copies, waits for them, and re-layouts: none -> 1.85 us  [spread(): copies = jnp.broadcast_to(value[None], (count,) + value.shape)]
    concatenate x1 -> x0, other arithmetic: 1.63 us -> none  [body(): own = jnp.concatenate([key_proj[0], value_proj[0]], axis=1)]
  transfers between devices with their start and end apart: 2 -> 1, of which waited for: 1 -> 0; matrix products, arithmetic and copies ran while one was open for 3% -> 1% of each run, Pallas kernels for 0% -> 2%
where the time goes in v3:
time: 105 us
  blocking collectives  86.5 us (82%)
  Pallas kernels  8.66 us (8%)
  starting transfers between devices  6.37 us (6%)
  local copies, waits for them, and re-layouts  1.86 us (2%)
  other arithmetic  1.27 us (1%)
    all_gather x1, blocking collectives, body(): lax.all_gather(packed, KEY_AXES, axis=0, tiled=True).astype(jnp.bfloat16)  49 us
    all_to_all x1, blocking collectives, body(): lax.all_to_all(shares, HEAD_AXES, split_axis=0, concat_axis=0, tiled=True)  22.6 us
    all_to_all x1, blocking collectives, body(): lax.all_to_all(partial, ROW_AXES, split_axis=0, concat_axis=0, tiled=True)  14.9 us
    all_to_all x1, starting transfers between devices, spread(): return lax.all_to_all(copies, axes, split_axis=0, concat_axis=0, tiled=True)  6.37 us
    pallas_call x1, Pallas kernels, attend(): pl.pallas_call(attend_kernel, grid=(heads,), out_shape=jax.ShapeDtypeStru...  3.6 us
  transfers between devices with their start and end apart: 1, of which 0 were waited for; matrix products, arithmetic and copies ran while one was open for 1% of the time, Pallas kernels for 2%

profile of v3, /device:TPU:1, one launch (start us, length us, event | category | flops | bytes accessed | tf_op | source)
XLA Modules:
  0.0 104.7 jit_solution(13233407750927682232)
XLA Ops:
  0.0 1.9 %broadcast_in_dim.11 = bf16[8,128,384]{2,1,0:T(8,128)(2,1)} broadcast(bf16[128,384]{1,0:T(8,128)(2,1)} %bitcast.7), dimensions={1,2} | broadcast | bytes 884736 | tf_op jit(solution)/shard_map/broadcast_in_dim | solution.py:177
  1.9 6.4 %all-to-all-start = ((bf16[8,128,384]{2,1,0:T(8,128)(2,1)}), bf16[8,128,384]{2,1,0:T(8,128)(2,1)S(1)}, u32[]{:S(2)}, u32[]{:S(2)}) async-start(bf16[8,128,384]{2,1,0:T(8,128)(2,1)} %broadcast_in_dim.11), calls=%async_computation | async-start | bytes 1572864 | tf_op jit(solution)/shard_map/all_to_all | solution.py:178
  8.2 1.8 %shard_map.46 = bf16[128,896]{1,0:T(8,128)(2,1)} custom-call(bf16[128,384]{1,0:T(8,128)(2,1)} %bitcast.8, bf16[128,384]{1,0:T(8,128)(2,1)} %bitcast.9), custom_call_target="tpu_custom_call" | custom-call | flops 196608 | bytes 393216 | tf_op jit(solution)/shard_map/pallas_call | solution.py:36
  10.0 1.0 convert_element_type.6
  11.0 49.0 %all-gather.1 = f16[1024,896]{1,0:T(8,128)(2,1)S(1)} all-gather(f16[128,896]{1,0:T(8,128)(2,1)S(1)} %convert_element_type.6), channel_id=1, replica_groups=mesh['branch'=2,'y'=4,'z2'=2,'z1'=2,'z0'=2,'x'=4,'core'=2] {'branch','z2..., dimensions={0}, use_global_device_ids=true | all-gather | bytes 2064384 | tf_op jit(solution)/shard_map/all_gather | solution.py:184
  60.0 0.3 convert_element_type.7.k_ref.v_ref.power_ref
  60.3 0.0 all-to-all-done
  60.3 0.0 copy-start
  60.3 3.6 %shard_map.47 = bf16[8,400,128]{2,1,0:T(8,128)(2,1)S(1)} custom-call(s32[1]{0:T(128)} %bitcast.edit_ref, bf16[1024,384]{1,0:T(8,128)(2,1)S(1)} %bitcast.6, bf16[1024,896]{1,0:T(8,128)(2,1)S(1)} %convert_element_type.7.k_ref.v_ref.power_ref, bf16[1024,896]{1,0:T(8,128)(2,1)S(1)} %convert_element_type.7.k_ref.v_ref.power_ref, ...), custom_call_target="tpu_custom_call" | custom-call | flops 1610612736 | bytes 3145728 | tf_op jit(solution)/shard_map/pallas_call | solution.py:94
  63.9 14.9 %all_to_all.15.parts_ref = bf16[8,400,128]{2,1,0:T(8,128)(2,1)S(1)} all-to-all(bf16[8,400,128]{2,1,0:T(8,128)(2,1)S(1)} %shard_map.47), channel_id=1, replica_groups=mesh['branch'=2,'y'=4,'z2'=2,'z1'=2,'z0'=2,'x'=4,'core'=2] {'y','z0'}, dimensions={0} | all-to-all | bytes 1638400 | tf_op jit(solution)/shard_map/all_to_all | solution.py:187
  78.8 0.0 copy-done
  78.8 1.4 %shard_map.48 = bf16[8,128,384]{2,1,0:T(8,128)(2,1)S(1)} custom-call(bf16[8,400,128]{2,1,0:T(8,128)(2,1)S(1)} %all_to_all.15.parts_ref, bf16[384,3072]{1,0:T(8,128)(2,1)S(1)} %copy-done), custom_call_target="tpu_custom_call" | custom-call | flops 301989888 | bytes 3178496 | tf_op jit(solution)/shard_map/pallas_call | solution.py:150
  80.2 22.6 %all_to_all.16.parts_ref = bf16[8,128,384]{2,1,0:T(8,128)(2,1)} all-to-all(bf16[8,128,384]{2,1,0:T(8,128)(2,1)S(1)} %shard_map.48), channel_id=1, replica_groups=mesh['branch'=2,'y'=4,'z2'=2,'z1'=2,'z0'=2,'x'=4,'core'=2] {'x','core'}, dimensions={0} | all-to-all | bytes 1572864 | tf_op jit(solution)/shard_map/all_to_all | solution.py:189
  102.8 1.9 %shard_map.49 = bf16[128,384]{1,0:T(8,128)(2,1)} custom-call(bf16[8,128,384]{2,1,0:T(8,128)(2,1)} %all_to_all.16.parts_ref), custom_call_target="tpu_custom_call" | custom-call | tf_op jit(solution)/shard_map/pallas_call | solution.py:170
Async XLA Ops:
  1.9 58.4 %all-to-all-start = ((bf16[8,128,384]{2,1,0:T(8,128)(2,1)}), bf16[8,128,384]{2,1,0:T(8,128)(2,1)S(1)}, u32[]{:S(2)}, u32[]{:S(2)}) async-start(bf16[8,128,384]{2,1,0:T(8,128)(2,1)} %broadcast_in_dim.11), calls=%async_computation | async-start | bytes 1572864 | tf_op jit(solution)/shard_map/all_to_all | solution.py:178
  60.3 18.5 %copy-start = (bf16[384,3072]{1,0:T(8,128)(2,1)S(1)}, bf16[384,3072]{1,0:T(8,128)(2,1)}, u32[]{:S(2)}) copy-start(bf16[384,3072]{1,0:T(8,128)(2,1)} %weight_ref.1) | copy-start | bytes 7077892

commit v4 on v3

--- a/solution.py
+++ b/solution.py
@@ -17,7 +17,9 @@
 HEAD_AXES = ("x", "core")
 
 
-def pack_kernel(key_ref, value_ref, out_ref):
+def pack_kernel(query_ref, key_ref, value_ref, out_ref, copies_ref):
+    for copy in range(copies_ref.shape[0]):
+        copies_ref[copy] = query_ref[...]
     feats = key_ref.shape[1]
     out_ref[:, :feats] = (key_ref[...].astype(jnp.float32) * 2.0**KEY_SHIFT).astype(jnp.bfloat16)
     values = value_ref[...].astype(jnp.float32)
@@ -31,22 +33,26 @@
     out_ref[:, 2 * feats :] = power.astype(jnp.bfloat16)
 
 
-def pack(keys, values):
+def pack(queries, keys, values, copies):
     rows, feats = keys.shape
     return pl.pallas_call(
         pack_kernel,
-        out_shape=jax.ShapeDtypeStruct((rows, 2 * feats + DH), jnp.bfloat16),
+        out_shape=(
+            jax.ShapeDtypeStruct((rows, 2 * feats + DH), jnp.bfloat16),
+            jax.ShapeDtypeStruct((copies, rows, feats), jnp.bfloat16),
+        ),
         cost_estimate=pl.CostEstimate(
-            flops=4 * rows * feats, bytes_accessed=8 * rows * feats, transcendentals=2 * rows * DH
-        ),
-    )(keys, values)
-
-
-def attend_kernel(edit_ref, q_ref, k_ref, v_ref, power_ref, out_ref, wide_ref, tail_ref):
+            flops=4 * rows * feats, bytes_accessed=24 * rows * feats, transcendentals=2 * rows * DH
+        ),
+    )(queries, keys, values)
+
+
+def attend_kernel(q_ref, k_ref, v_ref, power_ref, out_ref, wide_ref, tail_ref):
     head = pl.program_id(0)
     heads = pl.num_programs(0)
     row_blocks = out_ref.shape[0]
     key_count = k_ref.shape[0]
+    edit = lax.axis_index("branch")
 
     def attend(count):
         keys = k_ref[:count, :]
@@ -68,11 +74,11 @@
             level = peak * SCALE_LOG2 + jnp.log2(total)
             tail_ref[block, pl.ds(head, 1), :] = level.T[:1, :]
 
-    @pl.when(edit_ref[0] == 1)
+    @pl.when(edit == 1)
     def _():
         attend(key_count)
 
-    @pl.when(edit_ref[0] != 1)
+    @pl.when(edit != 1)
     def _():
         attend(key_count // 2)
 
@@ -86,7 +92,7 @@
         out_ref[:, out_ref.shape[1] - TAIL :, :] = pieces.astype(jnp.bfloat16)
 
 
-def attend(edit, queries, packed):
+def attend(queries, packed):
     rows, feats = queries.shape
     keys = packed.shape[0]
     heads = feats // DH
@@ -96,7 +102,6 @@
         grid=(heads,),
         out_shape=jax.ShapeDtypeStruct((blocks, heads * BLOCK + TAIL, DH), jnp.bfloat16),
         in_specs=[
-            pl.BlockSpec(memory_space=pltpu.SMEM),
             pl.BlockSpec((rows, DH), lambda h: (0, h)),
             pl.BlockSpec((keys, DH), lambda h: (0, h)),
             pl.BlockSpec((keys, DH), lambda h: (0, heads + h)),
@@ -113,13 +118,13 @@
             bytes_accessed=2 * (2 * rows * feats + 2 * keys * feats),
             transcendentals=rows * keys * heads,
         ),
-    )(edit, queries, packed, packed, packed)
-
-
-def merge_kernel(parts_ref, weight_ref, out_ref):
+    )(queries, packed, packed, packed)
+
+
+def merge_kernel(parts_ref, weight_ref, own_ref, other_ref):
     count, height, _ = parts_ref.shape
     heads = (height - TAIL) // BLOCK
-    columns = out_ref.shape[2]
+    targets, _, columns = own_ref.shape
     tail = parts_ref[:, height - TAIL :, :].astype(jnp.float32)
     level = tail[:, :4, :] + tail[:, 4:8, :] + tail[:, 8:12, :]
     share = jnp.exp2(level - jnp.max(level, axis=0, keepdims=True))
@@ -137,19 +142,29 @@
             total = total + values * turned[:, column : column + 1]
         merged.append(total.astype(jnp.bfloat16))
     attended = jnp.concatenate(merged, axis=1)
-    for target in range(out_ref.shape[0]):
-        out_ref[target] = jnp.dot(
+
+    def project(block):
+        return jnp.dot(
             attended,
-            weight_ref[:, target * columns : (target + 1) * columns],
+            weight_ref[:, block * columns : (block + 1) * columns],
             preferred_element_type=jnp.float32,
         ).astype(jnp.bfloat16)
 
+    for core in range(2):
+
+        @pl.when(lax.axis_index("core") == core)
+        def _():
+            for target in range(targets):
+                own_ref[target] = project(2 * target + core)
+                other_ref[target] = project(2 * target + 1 - core)
+
 
 def merge(parts, weight, targets):
-    columns = weight.shape[1] // targets
+    columns = weight.shape[1] // (2 * targets)
+    half = jax.ShapeDtypeStruct((targets, BLOCK, columns), jnp.bfloat16)
     return pl.pallas_call(
         merge_kernel,
-        out_shape=jax.ShapeDtypeStruct((targets, BLOCK, columns), jnp.bfloat16),
+        out_shape=(half, half),
         compiler_params=pltpu.CompilerParams(vmem_limit_bytes=16 * 1024 * 1024),
         cost_estimate=pl.CostEstimate(
             flops=2 * BLOCK * weight.size,
@@ -159,35 +174,19 @@
     )(parts, weight)
 
 
-def add_kernel(parts_ref, out_ref):
-    total = parts_ref[0].astype(jnp.float32)
-    for part in range(1, parts_ref.shape[0]):
-        total = total + parts_ref[part].astype(jnp.float32)
-    out_ref[...] = total.astype(jnp.bfloat16)
-
-
-def add(parts):
-    return pl.pallas_call(
-        add_kernel, out_shape=jax.ShapeDtypeStruct(parts.shape[1:], jnp.bfloat16)
-    )(parts)
-
-
-def spread(value, axes):
-    count = lax.axis_size(axes)
-    copies = jnp.broadcast_to(value[None], (count,) + value.shape)
-    return lax.all_to_all(copies, axes, split_axis=0, concat_axis=0, tiled=True)
-
-
 def body(query_proj, key_proj, value_proj, out_weight):
-    queries = spread(query_proj[0], ROW_AXES).reshape(-1, query_proj.shape[2])
-    packed = pack(key_proj[0], value_proj[0]).astype(jnp.float16)
+    packed, copies = pack(query_proj[0], key_proj[0], value_proj[0], lax.axis_size(ROW_AXES))
+    queries = lax.all_to_all(copies, ROW_AXES, split_axis=0, concat_axis=0, tiled=True)
+    queries = queries.reshape(-1, queries.shape[2])
+    packed = packed.astype(jnp.float16)
     packed = lax.all_gather(packed, KEY_AXES, axis=0, tiled=True).astype(jnp.bfloat16)
-    edit = lax.axis_index("branch").astype(jnp.int32).reshape(1)
-    partial = attend(edit, queries, packed)
+    partial = attend(queries, packed)
     parts = lax.all_to_all(partial, ROW_AXES, split_axis=0, concat_axis=0, tiled=True)
-    shares = merge(parts, out_weight, lax.axis_size(HEAD_AXES))
-    shares = lax.all_to_all(shares, HEAD_AXES, split_axis=0, concat_axis=0, tiled=True)
-    return add(shares)[None]
+    own, other = merge(parts, out_weight, lax.axis_size("x"))
+    other = lax.ppermute(other, "core", [(0, 1), (1, 0)])
+    shares = (own.astype(jnp.float32) + other.astype(jnp.float32)).astype(jnp.bfloat16)
+    shares = lax.all_to_all(shares, "x", split_axis=0, concat_axis=0, tiled=True)
+    return shares.astype(jnp.float32).sum(axis=0).astype(jnp.bfloat16)[None]
 
 
 def solution(mesh):

time: 105 us -> 102 us (0.971)
  blocking collectives: 86.5 us -> 76.3 us
  starting transfers between devices: 6.37 us -> 14.8 us
  local copies, waits for them, and re-layouts: 1.86 us -> 0.01 us
  Pallas kernels: 8.66 us -> 7 us
  waiting for transfers between devices: 0.01 us -> 1.33 us
    all_to_all x1, blocking collectives: 22.6 us -> 10.2 us  [body(): lax.all_to_all(shares, 'x', split_axis=0, concat_axis=0, tiled=True)]
    ppermute x0 -> x1, starting transfers between devices: none -> 8.38 us  [body(): other = lax.ppermute(other, 'core', [(0, 1), (1, 0)])]
    all_gather x1, blocking collectives: 49 us -> 51 us  [body(): lax.all_gather(packed, KEY_AXES, axis=0, tiled=True).astype(jnp.bfloat16)]
    broadcast_in_dim x1 -> x0, local copies, waits for them, and re-layouts: 1.85 us -> none  [spread(): copies = jnp.broadcast_to(value[None], (count,) + value.shape)]
    pallas_call x3 -> x2, Pallas kernels: 5.06 us -> 3.39 us  [the longest x1 2.03 us: pack(): pl.pallas_call(pack_kernel, out_shape=(jax.ShapeDtypeStruct((rows, 2 * fe...]
    ppermute x0 -> x1, waiting for transfers between devices: none -> 1.33 us  [body(): other = lax.ppermute(other, 'core', [(0, 1), (1, 0)])]
  transfers between devices with their start and end apart: 1 -> 2, of which waited for: 0 -> 1; matrix products, arithmetic and copies ran while one was open for 1% -> 1% of each run, Pallas kernels for 2% -> 0%
where the time goes in v4:
time: 102 us; the launch traced here: 101 us
  blocking collectives  76.3 us (75%)
  starting transfers between devices  14.8 us (15%)
  Pallas kernels  7 us (7%)
  other arithmetic  2.08 us (2%)
  waiting for transfers between devices  1.33 us (1%)
    all_gather x1, blocking collectives, body(): lax.all_gather(packed, KEY_AXES, axis=0, tiled=True).astype(jnp.bfloat16)  51 us
    all_to_all x1, blocking collectives, body(): lax.all_to_all(partial, ROW_AXES, split_axis=0, concat_axis=0, tiled=True)  15.1 us
    all_to_all x1, blocking collectives, body(): lax.all_to_all(shares, 'x', split_axis=0, concat_axis=0, tiled=True)  10.2 us
    ppermute x1, starting transfers between devices, body(): other = lax.ppermute(other, 'core', [(0, 1), (1, 0)])  8.38 us
    all_to_all x1, starting transfers between devices, body(): lax.all_to_all(copies, ROW_AXES, split_axis=0, concat_axis=0, tiled=True)  6.37 us
    pallas_call x1, Pallas kernels, attend(): pl.pallas_call(attend_kernel, grid=(heads,), out_shape=jax.ShapeDtypeStru...  3.61 us
  transfers between devices with their start and end apart: 2, of which 1 were waited for; matrix products, arithmetic and copies ran while one was open for 1% of the time, Pallas kernels for 0%

profile of v4, /device:TPU:1, one launch (start us, length us, event | category | flops | bytes accessed | tf_op | source)
XLA Modules:
  0.0 101.5 jit_solution(2539757117330286146)
XLA Ops:
  0.0 2.0 %shard_map.46 = (bf16[128,896]{1,0:T(8,128)(2,1)}, bf16[8,128,384]{2,1,0:T(8,128)(2,1)}) custom-call(bf16[128,384]{1,0:T(8,128)(2,1)} %bitcast.6, bf16[128,384]{1,0:T(8,128)(2,1)} %bitcast.7, bf16[128,384]{1,0:T(8,128)(2,1)} %bitcast.8), custom_call_target="tpu_custom_call" | custom-call | flops 196608 | bytes 1179648 | tf_op jit(solution)/shard_map/pallas_call | solution.py:38
  2.0 6.4 %all-to-all-start = ((bf16[8,128,384]{2,1,0:T(8,128)(2,1)}), bf16[8,128,384]{2,1,0:T(8,128)(2,1)S(1)}, u32[]{:S(2)}, u32[]{:S(2)}) async-start(bf16[8,128,384]{2,1,0:T(8,128)(2,1)} %get-tuple-element.9), calls=%async_computation | async-start | bytes 1572864 | tf_op jit(solution)/shard_map/all_to_all | solution.py:179
  8.4 1.0 convert_element_type.17
  9.4 51.0 %all-gather.1 = f16[1024,896]{1,0:T(8,128)(2,1)S(1)} all-gather(f16[128,896]{1,0:T(8,128)(2,1)S(1)} %convert_element_type.17), channel_id=1, replica_groups=mesh['branch'=2,'y'=4,'z2'=2,'z1'=2,'z0'=2,'x'=4,'core'=2] {'branch','z2..., dimensions={0}, use_global_device_ids=true | all-gather | bytes 2064384 | tf_op jit(solution)/shard_map/all_gather | solution.py:182
  60.4 0.3 convert_element_type.18.k_ref.v_ref.power_ref
  60.7 0.0 all-to-all-done
  60.7 0.0 copy-start
  60.7 3.6 %shard_map.47 = bf16[8,400,128]{2,1,0:T(8,128)(2,1)S(1)} custom-call(bf16[1024,384]{1,0:T(8,128)(2,1)S(1)} %bitcast.5, bf16[1024,896]{1,0:T(8,128)(2,1)S(1)} %convert_element_type.18.k_ref.v_ref.power_ref, bf16[1024,896]{1,0:T(8,128)(2,1)S(1)} %convert_element_type.18.k_ref.v_ref.power_ref, bf16[1024,896]{1,0:T(8,128)(2,1)S(1)} %convert_element_type.18.k_ref.v_ref.power_ref), custom_call_target="tpu_custom_call" | custom-call | flops 1610612736 | bytes 3145728 | tf_op jit(solution)/shard_map/pallas_call | solution.py:100
  64.3 15.1 %all_to_all.15.parts_ref = bf16[8,400,128]{2,1,0:T(8,128)(2,1)S(1)} all-to-all(bf16[8,400,128]{2,1,0:T(8,128)(2,1)S(1)} %shard_map.47), channel_id=1, replica_groups=mesh['branch'=2,'y'=4,'z2'=2,'z1'=2,'z0'=2,'x'=4,'core'=2] {'y','z0'}, dimensions={0} | all-to-all | bytes 1638400 | tf_op jit(solution)/shard_map/all_to_all | solution.py:184
  79.4 0.0 copy-done
  79.4 1.4 %shard_map.48 = (bf16[4,128,384]{2,1,0:T(8,128)(2,1)S(1)}, bf16[4,128,384]{2,1,0:T(8,128)(2,1)S(1)}) custom-call(bf16[8,400,128]{2,1,0:T(8,128)(2,1)S(1)} %all_to_all.15.parts_ref, bf16[384,3072]{1,0:T(8,128)(2,1)S(1)} %copy-done), custom_call_target="tpu_custom_call" | custom-call | flops 301989888 | bytes 3178496 | tf_op jit(solution)/shard_map/pallas_call | solution.py:165
  80.8 8.4 %collective-permute-start = (bf16[4,128,384]{2,1,0:T(8,128)(2,1)S(1)}, bf16[4,128,384]{2,1,0:T(8,128)(2,1)S(1)}, u32[]{:S(2)}, u32[]{:S(2)}) collective-permute-start(bf16[4,128,384]{2,1,0:T(8,128)(2,1)S(1)} %get-tuple-element.12), channel_id=1, source_target_pairs={{0,1},{1,0},{2,3},{3,2},{4,5},{5,4},{6,7},{7,6},{8,9},{9,8},{10,11... | collective-permute-start | bytes 1179656 | tf_op jit(solution)/shard_map/ppermute | solution.py:186
  89.2 1.3 %collective-permute-done = bf16[4,128,384]{2,1,0:T(8,128)(2,1)S(1)} collective-permute-done((bf16[4,128,384]{2,1,0:T(8,128)(2,1)S(1)}, bf16[4,128,384]{2,1,0:T(8,128)(2,1)S(1)}, u32[]{:S(2)}, u32[]{:S(2)}) %collective-permute-start) | collective-permute-done | bytes 393248 | tf_op jit(solution)/shard_map/ppermute | solution.py:186
  90.5 0.1 add_convert_fusion
  90.6 10.2 %all_to_all.16 = bf16[4,128,384]{2,1,0:T(8,128)(2,1)S(1)} all-to-all(bf16[4,128,384]{2,1,0:T(8,128)(2,1)S(1)} %add_convert_fusion), channel_id=1, replica_groups=mesh['branch'=2,'y'=4,'z2'=2,'z1'=2,'z0'=2,'x'=4,'core'=2] {'x'}, dimensions={0} | all-to-all | bytes 786432 | tf_op jit(solution)/shard_map/all_to_all | solution.py:188
  100.8 0.7 reduce_sum.12
Async XLA Ops:
  2.0 58.6 %all-to-all-start = ((bf16[8,128,384]{2,1,0:T(8,128)(2,1)}), bf16[8,128,384]{2,1,0:T(8,128)(2,1)S(1)}, u32[]{:S(2)}, u32[]{:S(2)}) async-start(bf16[8,128,384]{2,1,0:T(8,128)(2,1)} %get-tuple-element.9), calls=%async_computation | async-start | bytes 1572864 | tf_op jit(solution)/shard_map/all_to_all | solution.py:179
  60.7 18.7 %copy-start = (bf16[384,3072]{1,0:T(8,128)(2,1)S(1)}, bf16[384,3072]{1,0:T(8,128)(2,1)}, u32[]{:S(2)}) copy-start(bf16[384,3072]{1,0:T(8,128)(2,1)} %weight_ref.1) | copy-start | bytes 7077892
  80.8 9.7 %collective-permute-start = (bf16[4,128,384]{2,1,0:T(8,128)(2,1)S(1)}, bf16[4,128,384]{2,1,0:T(8,128)(2,1)S(1)}, u32[]{:S(2)}, u32[]{:S(2)}) collective-permute-start(bf16[4,128,384]{2,1,0:T(8,128)(2,1)S(1)} %get-tuple-element.12), channel_id=1, source_target_pairs={{0,1},{1,0},{2,3},{3,2},{4,5},{5,4},{6,7},{7,6},{8,9},{9,8},{10,11... | collective-permute-start | bytes 1179656 | tf_op jit(solution)/shard_map/ppermute | solution.py:186

commit v5 on v4

v5 whole, which is shorter than its diff:
```python
import math

import jax
import jax.numpy as jnp
from jax import lax
from jax.experimental import pallas as pl
from jax.experimental.pallas import tpu as pltpu
from jax.sharding import Mesh, PartitionSpec as P

DH = 128
BLOCK = 128
SCALE_LOG2 = math.log2(math.e) / math.sqrt(DH)
TAIL = 16
KEY_AXES = ("branch", "z2", "z1")
ROW_AXES = ("y", "z0")
HEAD_AXES = ("x", "core")


def attend_kernel(q_ref, own_ref, *refs):
    up_refs, down_refs = refs[:4], refs[4:7]
    out_ref, keys_ref, wide_ref, tail_ref = refs[7:]
    row_blocks = out_ref.shape[0]
    feats = q_ref.shape[1]
    heads = feats // DH

    def place(block_ref, slot):
        rows = pl.ds(pl.multiple_of(slot * BLOCK, BLOCK), BLOCK)
        keys_ref[rows, :] = block_ref[:, :feats]
        for head in range(heads):
            wide_ref[head, rows, :DH] = block_ref[:, feats + head * DH : feats + (head + 1) * DH]

    def attend(count):
        for head in range(heads):
            wide_ref[head, :count, DH:] = jnp.ones((count, DH), jnp.bfloat16)
            lanes = slice(head * DH, (head + 1) * DH)
            for block in range(row_blocks):
                queries = q_ref[block * BLOCK : (block + 1) * BLOCK, lanes]
                scores = lax.dot_general(
                    queries,
                    keys_ref[:count, lanes],
                    (((1,), (1,)), ((), ())),
                    preferred_element_type=jnp.float32,
                )
                peak = jnp.max(scores, axis=1, keepdims=True)
                weights = jnp.exp2((scores - peak) * SCALE_LOG2).astype(jnp.bfloat16)
                both = jnp.dot(
                    weights, wide_ref[head, :count, :], preferred_element_type=jnp.float32
                )
                total = both[:, DH:]
                out_ref[block, head * BLOCK : (head + 1) * BLOCK, :] = (
                    both[:, :DH] / total
                ).astype(jnp.bfloat16)
                level = peak * SCALE_LOG2 + jnp.log2(total)
                tail_ref[block, head : head + 1, :] = level.T[:1, :]

    edit = lax.axis_index("branch")
    index = 2 * lax.axis_index("z2") + lax.axis_index("z1")

    @pl.when(edit == 1)
    def _():
        for slot, block_ref in enumerate((own_ref,) + tuple(up_refs) + tuple(down_refs)):
            place(block_ref, slot)
        attend(8 * BLOCK)

    @pl.when(edit != 1)
    def _():
        place(own_ref, index)
        for step in range(1, 4):

            @pl.when(index - step >= 0)
            def _():
                place(up_refs[step - 1], index - step)

            @pl.when(index + step < 4)
            def _():
                place(down_refs[step - 1], index + step)

        attend(4 * BLOCK)

    level = tail_ref[:, :4, :]
    high = level.astype(jnp.bfloat16).astype(jnp.float32)
    middle = (level - high).astype(jnp.bfloat16).astype(jnp.float32)
    low = level - high - middle
    pieces = jnp.concatenate([high, middle, low, jnp.zeros_like(low)], axis=1)
    out_ref[:, heads * BLOCK :, :] = pieces.astype(jnp.bfloat16)


def attend(queries, own, up, down):
    rows, feats = queries.shape
    keys = 8 * BLOCK
    heads = feats // DH
    blocks = rows // BLOCK
    return pl.pallas_call(
        attend_kernel,
        out_shape=jax.ShapeDtypeStruct((blocks, heads * BLOCK + TAIL, DH), jnp.bfloat16),
        scratch_shapes=[
            pltpu.VMEM((keys, feats), jnp.bfloat16),
            pltpu.VMEM((heads, keys, 2 * DH), jnp.bfloat16),
            pltpu.VMEM((blocks, 8, BLOCK), jnp.float32),
        ],
        compiler_params=pltpu.CompilerParams(vmem_limit_bytes=32 * 1024 * 1024),
        cost_estimate=pl.CostEstimate(
            flops=4 * rows * keys * feats,
            bytes_accessed=2 * (2 * rows * feats + 2 * keys * feats),
            transcendentals=rows * keys * heads,
        ),
    )(queries, own, *up, *down)


def merge_kernel(parts_ref, weight_ref, own_ref, other_ref):
    count, height, _ = parts_ref.shape
    heads = (height - TAIL) // BLOCK
    targets, _, columns = own_ref.shape
    tail = parts_ref[:, height - TAIL :, :].astype(jnp.float32)
    level = tail[:, :4, :] + tail[:, 4:8, :] + tail[:, 8:12, :]
    share = jnp.exp2(level - jnp.max(level, axis=0, keepdims=True))
    share = share / jnp.sum(share, axis=0, keepdims=True)
    flat = jnp.concatenate(
        [share.reshape(count * 4, BLOCK), jnp.zeros((BLOCK - count * 4, BLOCK), jnp.float32)], axis=0
    )
    turned = flat.T
    merged = []
    for head in range(heads):
        total = jnp.zeros((BLOCK, DH), jnp.float32)
        for part in range(count):
            column = part * 4 + head
            values = parts_ref[part, head * BLOCK : (head + 1) * BLOCK, :].astype(jnp.float32)
            total = total + values * turned[:, column : column + 1]
        merged.append(total.astype(jnp.bfloat16))
    attended = jnp.concatenate(merged, axis=1)

    def project(block):
        return jnp.dot(
            attended,
            weight_ref[:, block * columns : (block + 1) * columns],
            preferred_element_type=jnp.float32,
        ).astype(jnp.bfloat16)

    for core in range(2):

        @pl.when(lax.axis_index("core") == core)
        def _():
            for target in range(targets):
                own_ref[target] = project(2 * target + core)
                other_ref[target] = project(2 * target + 1 - core)


def merge(parts, weight, targets):
    columns = weight.shape[1] // (2 * targets)
    half = jax.ShapeDtypeStruct((targets, BLOCK, columns), jnp.bfloat16)
    return pl.pallas_call(
        merge_kernel,
        out_shape=(half, half),
        compiler_params=pltpu.CompilerParams(vmem_limit_bytes=16 * 1024 * 1024),
        cost_estimate=pl.CostEstimate(
            flops=2 * BLOCK * weight.size,
            bytes_accessed=2 * (parts.size + weight.size),
            transcendentals=0,
        ),
    )(parts, weight)


def spread(value, axes):
    count = lax.axis_size(axes)
    copies = jnp.broadcast_to(value[None], (count,) + value.shape)
    return lax.all_to_all(copies, axes, split_axis=0, concat_axis=0, tiled=True)


def ring_pairs(step, turn):
    pairs = []
    for sender in range(8):
        block = (sender - turn * (step - 1)) % 8
        target = (sender + turn) % 8
        if block < 4 or (sender >= 4 and target >= 4):
            pairs.append((sender, target))
    return pairs


def body(query_proj, key_proj, value_proj, out_weight):
    own = jnp.concatenate([key_proj[0], value_proj[0]], axis=1)
    query = query_proj[0]
    beside = lax.ppermute(query, "z0", [(0, 1), (1, 0)])
    up, down = [own], [own]
    for step in range(1, 5):
        up.append(lax.ppermute(up[-1], KEY_AXES, ring_pairs(step, 1)))
        if step < 4:
            down.append(lax.ppermute(down[-1], KEY_AXES, ring_pairs(step, -1)))
        if step == 1:
            beside, up[1] = lax.optimization_barrier((beside, up[1]))
            first = lax.axis_index("z0") == 0
            pair = jnp.concatenate(
                [jnp.where(first, query, beside), jnp.where(first, beside, query)], axis=0
            )
            queries = spread(pair, "y").reshape(-1, query.shape[1])
    partial = attend(queries, own, up[1:], down[1:])
    parts = lax.all_to_all(partial, ROW_AXES, split_axis=0, concat_axis=0, tiled=True)
    own, other = merge(parts, out_weight, lax.axis_size("x"))
    other = lax.ppermute(other, "core", [(0, 1), (1, 0)])
    shares = (own.astype(jnp.float32) + other.astype(jnp.float32)).astype(jnp.bfloat16)
    shares = lax.all_to_all(shares, "x", split_axis=0, concat_axis=0, tiled=True)
    return shares.astype(jnp.float32).sum(axis=0).astype(jnp.bfloat16)[None]


def solution(mesh):
    split = Mesh(
        mesh.devices.reshape(2, 4, 2, 2, 2, 4, 2),
        ("branch", "y", "z2", "z1", "z0", "x", "core"),
    )
    rows = ("y", "z2", "z1", "z0")
    placed = P("branch", rows, HEAD_AXES)
    return jax.shard_map(
        body,
        mesh=split,
        in_specs=(placed, placed, placed, P(HEAD_AXES, None)),
        out_specs=placed,
        check_vma=False,
    )
```

time: 102 us -> 95.7 us (0.938)
  the two profiles are of different devices: /device:TPU:1 before, /device:TPU:448 now
where the time goes in v5:
time: 95.7 us; the launch traced here: 95.2 us
  blocking collectives  30.8 us (32%)
  starting transfers between devices  30.4 us (32%)
  waiting for transfers between devices  24.4 us (25%)
  Pallas kernels  5.78 us (6%)
  other arithmetic  2.7 us (3%)
  local copies, waits for them, and re-layouts  0.96 us (1%)
    all_to_all x1, blocking collectives, body(): lax.all_to_all(partial, ROW_AXES, split_axis=0, concat_axis=0, tiled=True)  18.3 us
    ppermute x3, starting transfers between devices, body(): down.append(lax.ppermute(down[-1], KEY_AXES, ring_pairs(step, -1)))  16 us
    all_to_all x1, blocking collectives, body(): lax.all_to_all(shares, 'x', split_axis=0, concat_axis=0, tiled=True)  12.5 us
    ppermute x3, waiting for transfers between devices, body(): down.append(lax.ppermute(down[-1], KEY_AXES, ring_pairs(step, -1)))  11.6 us
    ppermute x4, waiting for transfers between devices, body(): up.append(lax.ppermute(up[-1], KEY_AXES, ring_pairs(step, 1)))  11 us
    ppermute x4, starting transfers between devices, body(): up.append(lax.ppermute(up[-1], KEY_AXES, ring_pairs(step, 1)))  5.16 us
    all_to_all x1, starting transfers between devices, spread(): return lax.all_to_all(copies, axes, split_axis=0, concat_axis=0, tiled=True)  4.46 us
    pallas_call x1, Pallas kernels, attend(): pl.pallas_call(attend_kernel, out_shape=jax.ShapeDtypeStruct((blocks, hea...  4.42 us
  transfers between devices with their start and end apart: 10, of which 5 were waited for; matrix products, arithmetic and copies ran while one was open for 2% of the time, Pallas kernels for 0%

profile of v5, /device:TPU:448, one launch (start us, length us, event | category | flops | bytes accessed | tf_op | source)
XLA Modules:
  0.0 95.2 jit_solution(14418515887816488309)
XLA Ops:
  0.0 1.0 %pad_maximum_fusion.own_ref = bf16[128,768]{1,0:T(8,128)(2,1)S(1)} fusion(bf16[128,384]{1,0:T(8,128)(2,1)} %bitcast.8, bf16[128,384]{1,0:T(8,128)(2,1)} %bitcast.9), kind=kLoop, calls=%fused_computation.1 | loop fusion | flops 393216 | bytes 393216 | tf_op jit(solution)/shard_map/concatenate | solution.py:180
  1.0 1.3 %collective-permute-start.1 = (bf16[128,768]{1,0:T(8,128)(2,1)S(1)}, bf16[128,768]{1,0:T(8,128)(2,1)S(1)}, u32[]{:S(2)}, u32[]{:S(2)}) collective-permute-start(bf16[128,768]{1,0:T(8,128)(2,1)S(1)} %pad_maximum_fusion.own_ref), channel_id=1, source_target_pairs={{0,16},{16,32},{32,48},{48,256},{256,272},{272,288},{288,304},{1,1... | collective-permute-start | bytes 589832 | tf_op jit(solution)/shard_map/ppermute | solution.py:185
  2.3 2.9 %collective-permute-start = (bf16[128,384]{1,0:T(8,128)(2,1)}, bf16[128,384]{1,0:T(8,128)(2,1)S(1)}, u32[]{:S(2)}, u32[]{:S(2)}) collective-permute-start(bf16[128,384]{1,0:T(8,128)(2,1)} %bitcast.10), channel_id=1, source_target_pairs={{0,8},{8,0},{1,9},{9,1},{2,10},{10,2},{3,11},{11,3},{4,12},{12,4},... | collective-permute-start | bytes 294920 | tf_op jit(solution)/shard_map/ppermute | solution.py:182
  5.2 5.4 %collective-permute-start.5 = (bf16[128,768]{1,0:T(8,128)(2,1)S(1)}, bf16[128,768]{1,0:T(8,128)(2,1)S(1)}, u32[]{:S(2)}, u32[]{:S(2)}) collective-permute-start(bf16[128,768]{1,0:T(8,128)(2,1)S(1)} %pad_maximum_fusion.own_ref), channel_id=1, source_target_pairs={{0,304},{16,0},{32,16},{48,32},{272,256},{288,272},{304,288},{1,30... | collective-permute-start | bytes 589832 | tf_op jit(solution)/shard_map/ppermute | solution.py:187
  10.7 0.0 collective-permute-done
  10.7 5.0 %collective-permute-done.1.refs_0_ = bf16[128,768]{1,0:T(8,128)(2,1)S(1)} collective-permute-done((bf16[128,768]{1,0:T(8,128)(2,1)S(1)}, bf16[128,768]{1,0:T(8,128)(2,1)S(1)}, u32[]{:S(2)}, u32[]{:S(2)}) %collective-permute-start.1) | collective-permute-done | bytes 196640 | tf_op jit(solution)/shard_map/ppermute | solution.py:185
  15.7 1.3 %collective-permute-start.2 = (bf16[128,768]{1,0:T(8,128)(2,1)S(1)}, bf16[128,768]{1,0:T(8,128)(2,1)S(1)}, u32[]{:S(2)}, u32[]{:S(2)}) collective-permute-start(bf16[128,768]{1,0:T(8,128)(2,1)S(1)} %collective-permute-done.1.refs_0_), channel_id=1, source_target_pairs={{16,32},{32,48},{48,256},{256,272},{272,288},{288,304},{17,33},{33... | collective-permute-start | bytes 589832 | tf_op jit(solution)/shard_map/ppermute | solution.py:185
  17.0 0.9 broadcast_select_fusion.1
  17.9 1.0 %broadcast_in_dim.4 = bf16[4,256,384]{2,1,0:T(8,128)(2,1)} broadcast(bf16[256,384]{1,0:T(8,128)(2,1)S(1)} %pad_maximum_fusion.1), dimensions={1,2} | broadcast | bytes 983040 | tf_op jit(solution)/shard_map/broadcast_in_dim | solution.py:165
  18.9 4.5 %all-to-all-start = ((bf16[4,256,384]{2,1,0:T(8,128)(2,1)}), bf16[4,256,384]{2,1,0:T(8,128)(2,1)S(1)}, u32[]{:S(2)}, u32[]{:S(2)}) async-start(bf16[4,256,384]{2,1,0:T(8,128)(2,1)} %broadcast_in_dim.4), calls=%async_computation | async-start | bytes 1572864 | tf_op jit(solution)/shard_map/all_to_all | solution.py:166
  23.4 0.0 collective-permute-done.5.refs_4_
  23.4 5.4 %collective-permute-start.6 = (bf16[128,768]{1,0:T(8,128)(2,1)S(1)}, bf16[128,768]{1,0:T(8,128)(2,1)S(1)}, u32[]{:S(2)}, u32[]{:S(2)}) collective-permute-start(bf16[128,768]{1,0:T(8,128)(2,1)S(1)} %collective-permute-done.5.refs_4_), channel_id=1, source_target_pairs={{0,304},{16,0},{32,16},{272,256},{288,272},{304,288},{1,305},{17,1... | collective-permute-start | bytes 589832 | tf_op jit(solution)/shard_map/ppermute | solution.py:187
  28.8 0.0 collective-permute-done.2.refs_1_
  28.8 1.3 %collective-permute-start.3 = (bf16[128,768]{1,0:T(8,128)(2,1)S(1)}, bf16[128,768]{1,0:T(8,128)(2,1)S(1)}, u32[]{:S(2)}, u32[]{:S(2)}) collective-permute-start(bf16[128,768]{1,0:T(8,128)(2,1)S(1)} %collective-permute-done.2.refs_1_), channel_id=1, source_target_pairs={{32,48},{48,256},{256,272},{272,288},{288,304},{33,49},{49,257},{2... | collective-permute-start | bytes 589832 | tf_op jit(solution)/shard_map/ppermute | solution.py:185
  30.1 5.4 %collective-permute-done.6.refs_5_ = bf16[128,768]{1,0:T(8,128)(2,1)S(1)} collective-permute-done((bf16[128,768]{1,0:T(8,128)(2,1)S(1)}, bf16[128,768]{1,0:T(8,128)(2,1)S(1)}, u32[]{:S(2)}, u32[]{:S(2)}) %collective-permute-start.6) | collective-permute-done | bytes 196640 | tf_op jit(solution)/shard_map/ppermute | solution.py:187
  35.5 5.1 %collective-permute-start.7 = (bf16[128,768]{1,0:T(8,128)(2,1)S(1)}, bf16[128,768]{1,0:T(8,128)(2,1)S(1)}, u32[]{:S(2)}, u32[]{:S(2)}) collective-permute-start(bf16[128,768]{1,0:T(8,128)(2,1)S(1)} %collective-permute-done.6.refs_5_), channel_id=1, source_target_pairs={{0,304},{16,0},{272,256},{288,272},{304,288},{1,305},{17,1},{273,2... | collective-permute-start | bytes 589832 | tf_op jit(solution)/shard_map/ppermute | solution.py:187
  40.6 0.0 collective-permute-done.3.refs_2_
  40.6 1.3 %collective-permute-start.4 = (bf16[128,768]{1,0:T(8,128)(2,1)S(1)}, bf16[128,768]{1,0:T(8,128)(2,1)S(1)}, u32[]{:S(2)}, u32[]{:S(2)}) collective-permute-start(bf16[128,768]{1,0:T(8,128)(2,1)S(1)} %collective-permute-done.3.refs_2_), channel_id=1, source_target_pairs={{48,256},{256,272},{272,288},{288,304},{49,257},{257,273},{273,289... | collective-permute-start | bytes 589832 | tf_op jit(solution)/shard_map/ppermute | solution.py:185
  41.9 6.3 %collective-permute-done.7.refs_6_ = bf16[128,768]{1,0:T(8,128)(2,1)S(1)} collective-permute-done((bf16[128,768]{1,0:T(8,128)(2,1)S(1)}, bf16[128,768]{1,0:T(8,128)(2,1)S(1)}, u32[]{:S(2)}, u32[]{:S(2)}) %collective-permute-start.7) | collective-permute-done | bytes 196640 | tf_op jit(solution)/shard_map/ppermute | solution.py:187
  48.2 6.0 %collective-permute-done.4.refs_3_ = bf16[128,768]{1,0:T(8,128)(2,1)S(1)} collective-permute-done((bf16[128,768]{1,0:T(8,128)(2,1)S(1)}, bf16[128,768]{1,0:T(8,128)(2,1)S(1)}, u32[]{:S(2)}, u32[]{:S(2)}) %collective-permute-start.4) | collective-permute-done | bytes 196640 | tf_op jit(solution)/shard_map/ppermute | solution.py:185
  54.2 0.0 all-to-all-done
  54.2 0.0 copy-start
  54.2 4.4 %shard_map.46 = bf16[8,400,128]{2,1,0:T(8,128)(2,1)S(1)} custom-call(bf16[1024,384]{1,0:T(8,128)(2,1)S(1)} %bitcast.7, bf16[128,768]{1,0:T(8,128)(2,1)S(1)} %pad_maximum_fusion.own_ref, bf16[128,768]{1,0:T(8,128)(2,1)S(1)} %collective-permute-done.1.refs_0_, bf16[128,768]{1,0:T(8,128)(2,1)S(1)} %collective-permute-done.2.refs_1_, ...), custom_call_target="tpu_custom_call" | custom-call | flops 1610612736 | bytes 3145728 | tf_op jit(solution)/shard_map/pallas_call | solution.py:93
  58.6 18.3 %all_to_all.15.parts_ref = bf16[8,400,128]{2,1,0:T(8,128)(2,1)S(1)} all-to-all(bf16[8,400,128]{2,1,0:T(8,128)(2,1)S(1)} %shard_map.46), channel_id=1, replica_groups=mesh['branch'=2,'y'=4,'z2'=2,'z1'=2,'z0'=2,'x'=4,'core'=2] {'y','z0'}, dimensions={0} | all-to-all | bytes 1638400 | tf_op jit(solution)/shard_map/all_to_all | solution.py:196
  76.9 0.0 copy-done
  76.9 1.4 %shard_map.47 = (bf16[4,128,384]{2,1,0:T(8,128)(2,1)S(1)}, bf16[4,128,384]{2,1,0:T(8,128)(2,1)S(1)}) custom-call(bf16[8,400,128]{2,1,0:T(8,128)(2,1)S(1)} %all_to_all.15.parts_ref, bf16[384,3072]{1,0:T(8,128)(2,1)S(1)} %copy-done), custom_call_target="tpu_custom_call" | custom-call | flops 301989888 | bytes 3178496 | tf_op jit(solution)/shard_map/pallas_call | solution.py:151
  78.3 1.9 %collective-permute-start.8 = (bf16[4,128,384]{2,1,0:T(8,128)(2,1)S(1)}, bf16[4,128,384]{2,1,0:T(8,128)(2,1)S(1)}, u32[]{:S(2)}, u32[]{:S(2)}) collective-permute-start(bf16[4,128,384]{2,1,0:T(8,128)(2,1)S(1)} %get-tuple-element.12), channel_id=1, source_target_pairs={{0,1},{1,0},{2,3},{3,2},{4,5},{5,4},{6,7},{7,6},{8,9},{9,8},{10,11... | collective-permute-start | bytes 1179656 | tf_op jit(solution)/shard_map/ppermute | solution.py:198
  80.2 1.7 %collective-permute-done.8 = bf16[4,128,384]{2,1,0:T(8,128)(2,1)S(1)} collective-permute-done((bf16[4,128,384]{2,1,0:T(8,128)(2,1)S(1)}, bf16[4,128,384]{2,1,0:T(8,128)(2,1)S(1)}, u32[]{:S(2)}, u32[]{:S(2)}) %collective-permute-start.8) | collective-permute-done | bytes 393248 | tf_op jit(solution)/shard_map/ppermute | solution.py:198
  81.9 0.1 add_convert_fusion
  82.0 12.5 %all_to_all.16 = bf16[4,128,384]{2,1,0:T(8,128)(2,1)S(1)} all-to-all(bf16[4,128,384]{2,1,0:T(8,128)(2,1)S(1)} %add_convert_fusion), channel_id=1, replica_groups=mesh['branch'=2,'y'=4,'z2'=2,'z1'=2,'z0'=2,'x'=4,'core'=2] {'x'}, dimensions={0} | all-to-all | bytes 786432 | tf_op jit(solution)/shard_map/all_to_all | solution.py:200
  94.5 0.7 reduce_sum.12
  (1 shorter events, 0.0 us)
Async XLA Ops:
  1.0 14.7 %collective-permute-start.1 = (bf16[128,768]{1,0:T(8,128)(2,1)S(1)}, bf16[128,768]{1,0:T(8,128)(2,1)S(1)}, u32[]{:S(2)}, u32[]{:S(2)}) collective-permute-start(bf16[128,768]{1,0:T(8,128)(2,1)S(1)} %pad_maximum_fusion.own_ref), channel_id=1, source_target_pairs={{0,16},{16,32},{32,48},{48,256},{256,272},{272,288},{288,304},{1,1... | collective-permute-start | bytes 589832 | tf_op jit(solution)/shard_map/ppermute | solution.py:185
  2.3 8.4 %collective-permute-start = (bf16[128,384]{1,0:T(8,128)(2,1)}, bf16[128,384]{1,0:T(8,128)(2,1)S(1)}, u32[]{:S(2)}, u32[]{:S(2)}) collective-permute-start(bf16[128,384]{1,0:T(8,128)(2,1)} %bitcast.10), channel_id=1, source_target_pairs={{0,8},{8,0},{1,9},{9,1},{2,10},{10,2},{3,11},{11,3},{4,12},{12,4},... | collective-permute-start | bytes 294920 | tf_op jit(solution)/shard_map/ppermute | solution.py:182
  5.2 18.2 %collective-permute-start.5 = (bf16[128,768]{1,0:T(8,128)(2,1)S(1)}, bf16[128,768]{1,0:T(8,128)(2,1)S(1)}, u32[]{:S(2)}, u32[]{:S(2)}) collective-permute-start(bf16[128,768]{1,0:T(8,128)(2,1)S(1)} %pad_maximum_fusion.own_ref), channel_id=1, source_target_pairs={{0,304},{16,0},{32,16},{48,32},{272,256},{288,272},{304,288},{1,30... | collective-permute-start | bytes 589832 | tf_op jit(solution)/shard_map/ppermute | solution.py:187
  15.7 13.1 %collective-permute-start.2 = (bf16[128,768]{1,0:T(8,128)(2,1)S(1)}, bf16[128,768]{1,0:T(8,128)(2,1)S(1)}, u32[]{:S(2)}, u32[]{:S(2)}) collective-permute-start(bf16[128,768]{1,0:T(8,128)(2,1)S(1)} %collective-permute-done.1.refs_0_), channel_id=1, source_target_pairs={{16,32},{32,48},{48,256},{256,272},{272,288},{288,304},{17,33},{33... | collective-permute-start | bytes 589832 | tf_op jit(solution)/shard_map/ppermute | solution.py:185
  18.9 35.3 %all-to-all-start = ((bf16[4,256,384]{2,1,0:T(8,128)(2,1)}), bf16[4,256,384]{2,1,0:T(8,128)(2,1)S(1)}, u32[]{:S(2)}, u32[]{:S(2)}) async-start(bf16[4,256,384]{2,1,0:T(8,128)(2,1)} %broadcast_in_dim.4), calls=%async_computation | async-start | bytes 1572864 | tf_op jit(solution)/shard_map/all_to_all | solution.py:166
  23.4 12.1 %collective-permute-start.6 = (bf16[128,768]{1,0:T(8,128)(2,1)S(1)}, bf16[128,768]{1,0:T(8,128)(2,1)S(1)}, u32[]{:S(2)}, u32[]{:S(2)}) collective-permute-start(bf16[128,768]{1,0:T(8,128)(2,1)S(1)} %collective-permute-done.5.refs_4_), channel_id=1, source_target_pairs={{0,304},{16,0},{32,16},{272,256},{288,272},{304,288},{1,305},{17,1... | collective-permute-start | bytes 589832 | tf_op jit(solution)/shard_map/ppermute | solution.py:187
  28.8 11.8 %collective-permute-start.3 = (bf16[128,768]{1,0:T(8,128)(2,1)S(1)}, bf16[128,768]{1,0:T(8,128)(2,1)S(1)}, u32[]{:S(2)}, u32[]{:S(2)}) collective-permute-start(bf16[128,768]{1,0:T(8,128)(2,1)S(1)} %collective-permute-done.2.refs_1_), channel_id=1, source_target_pairs={{32,48},{48,256},{256,272},{272,288},{288,304},{33,49},{49,257},{2... | collective-permute-start | bytes 589832 | tf_op jit(solution)/shard_map/ppermute | solution.py:185
  35.5 12.7 %collective-permute-start.7 = (bf16[128,768]{1,0:T(8,128)(2,1)S(1)}, bf16[128,768]{1,0:T(8,128)(2,1)S(1)}, u32[]{:S(2)}, u32[]{:S(2)}) collective-permute-start(bf16[128,768]{1,0:T(8,128)(2,1)S(1)} %collective-permute-done.6.refs_5_), channel_id=1, source_target_pairs={{0,304},{16,0},{272,256},{288,272},{304,288},{1,305},{17,1},{273,2... | collective-permute-start | bytes 589832 | tf_op jit(solution)/shard_map/ppermute | solution.py:187
  40.6 13.6 %collective-permute-start.4 = (bf16[128,768]{1,0:T(8,128)(2,1)S(1)}, bf16[128,768]{1,0:T(8,128)(2,1)S(1)}, u32[]{:S(2)}, u32[]{:S(2)}) collective-permute-start(bf16[128,768]{1,0:T(8,128)(2,1)S(1)} %collective-permute-done.3.refs_2_), channel_id=1, source_target_pairs={{48,256},{256,272},{272,288},{288,304},{49,257},{257,273},{273,289... | collective-permute-start | bytes 589832 | tf_op jit(solution)/shard_map/ppermute | solution.py:185
  54.2 22.7 %copy-start = (bf16[384,3072]{1,0:T(8,128)(2,1)S(1)}, bf16[384,3072]{1,0:T(8,128)(2,1)}, u32[]{:S(2)}) copy-start(bf16[384,3072]{1,0:T(8,128)(2,1)} %weight_ref.1) | copy-start | bytes 7077892
  78.3 3.6 %collective-permute-start.8 = (bf16[4,128,384]{2,1,0:T(8,128)(2,1)S(1)}, bf16[4,128,384]{2,1,0:T(8,128)(2,1)S(1)}, u32[]{:S(2)}, u32[]{:S(2)}) collective-permute-start(bf16[4,128,384]{2,1,0:T(8,128)(2,1)S(1)} %get-tuple-element.12), channel_id=1, source_target_pairs={{0,1},{1,0},{2,3},{3,2},{4,5},{5,4},{6,7},{7,6},{8,9},{9,8},{10,11... | collective-permute-start | bytes 1179656 | tf_op jit(solution)/shard_map/ppermute | solution.py:198

commit v6 on v5

--- a/solution.py
+++ b/solution.py
@@ -34,6 +34,7 @@
             wide_ref[head, :count, DH:] = jnp.ones((count, DH), jnp.bfloat16)
             lanes = slice(head * DH, (head + 1) * DH)
             for block in range(row_blocks):
+                target = block // 2 * 2 + (block % 2 ^ side)
                 queries = q_ref[block * BLOCK : (block + 1) * BLOCK, lanes]
                 scores = lax.dot_general(
                     queries,
@@ -47,12 +48,13 @@
                     weights, wide_ref[head, :count, :], preferred_element_type=jnp.float32
                 )
                 total = both[:, DH:]
-                out_ref[block, head * BLOCK : (head + 1) * BLOCK, :] = (
+                out_ref[target, head * BLOCK : (head + 1) * BLOCK, :] = (
                     both[:, :DH] / total
                 ).astype(jnp.bfloat16)
                 level = peak * SCALE_LOG2 + jnp.log2(total)
-                tail_ref[block, head : head + 1, :] = level.T[:1, :]
-
+                tail_ref[target, head : head + 1, :] = level.T[:1, :]
+
+    side = lax.axis_index("z0")
     edit = lax.axis_index("branch")
     index = 2 * lax.axis_index("z2") + lax.axis_index("z1")
 
@@ -99,11 +101,7 @@
             pltpu.VMEM((blocks, 8, BLOCK), jnp.float32),
         ],
         compiler_params=pltpu.CompilerParams(vmem_limit_bytes=32 * 1024 * 1024),
-        cost_estimate=pl.CostEstimate(
-            flops=4 * rows * keys * feats,
-            bytes_accessed=2 * (2 * rows * feats + 2 * keys * feats),
-            transcendentals=rows * keys * heads,
-        ),
+        cost_estimate=pl.CostEstimate(flops=0, bytes_accessed=0, transcendentals=0),
     )(queries, own, *up, *down)
 
 
@@ -187,10 +185,7 @@
             down.append(lax.ppermute(down[-1], KEY_AXES, ring_pairs(step, -1)))
         if step == 1:
             beside, up[1] = lax.optimization_barrier((beside, up[1]))
-            first = lax.axis_index("z0") == 0
-            pair = jnp.concatenate(
-                [jnp.where(first, query, beside), jnp.where(first, beside, query)], axis=0
-            )
+            pair = jnp.concatenate([query, beside], axis=0)
             queries = spread(pair, "y").reshape(-1, query.shape[1])
     partial = attend(queries, own, up[1:], down[1:])
     parts = lax.all_to_all(partial, ROW_AXES, split_axis=0, concat_axis=0, tiled=True)

time: 95.7 us -> 95.6 us (level)
  no operation moved by 1% of the time
where the time goes in v6:
time: 95.6 us; the launch traced here: 95.1 us
  blocking collectives  30.6 us (32%)
  starting transfers between devices  30.4 us (32%)
  waiting for transfers between devices  24.5 us (26%)
  Pallas kernels  5.82 us (6%)
  other arithmetic  2.68 us (3%)
    all_to_all x1, blocking collectives, body(): lax.all_to_all(partial, ROW_AXES, split_axis=0, concat_axis=0, tiled=True)  18.2 us
    ppermute x3, starting transfers between devices, body(): down.append(lax.ppermute(down[-1], KEY_AXES, ring_pairs(step, -1)))  16 us
    all_to_all x1, blocking collectives, body(): lax.all_to_all(shares, 'x', split_axis=0, concat_axis=0, tiled=True)  12.5 us
    ppermute x3, waiting for transfers between devices, body(): down.append(lax.ppermute(down[-1], KEY_AXES, ring_pairs(step, -1)))  11.6 us
    ppermute x4, waiting for transfers between devices, body(): up.append(lax.ppermute(up[-1], KEY_AXES, ring_pairs(step, 1)))  11.1 us
    ppermute x4, starting transfers between devices, body(): up.append(lax.ppermute(up[-1], KEY_AXES, ring_pairs(step, 1)))  5.16 us
    all_to_all x1, starting transfers between devices, spread(): return lax.all_to_all(copies, axes, split_axis=0, concat_axis=0, tiled=True)  4.46 us
    pallas_call x1, Pallas kernels, attend(): pl.pallas_call(attend_kernel, out_shape=jax.ShapeDtypeStruct((blocks, hea...  4.46 us
  transfers between devices with their start and end apart: 10, of which 5 were waited for; matrix products, arithmetic and copies ran while one was open for 2% of the time, Pallas kernels for 0%

profile of v6, /device:TPU:448, one launch (start us, length us, event | category | flops | bytes accessed | tf_op | source)
XLA Modules:
  0.0 95.1 jit_solution(1581104044971533759)
XLA Ops:
  0.0 1.0 %pad_maximum_fusion.own_ref = bf16[128,768]{1,0:T(8,128)(2,1)S(1)} fusion(bf16[128,384]{1,0:T(8,128)(2,1)} %bitcast.6, bf16[128,384]{1,0:T(8,128)(2,1)} %bitcast.7), kind=kLoop, calls=%fused_computation.1 | loop fusion | flops 393216 | bytes 393216 | tf_op jit(solution)/shard_map/concatenate | solution.py:178
  1.0 1.3 %collective-permute-start.1 = (bf16[128,768]{1,0:T(8,128)(2,1)S(1)}, bf16[128,768]{1,0:T(8,128)(2,1)S(1)}, u32[]{:S(2)}, u32[]{:S(2)}) collective-permute-start(bf16[128,768]{1,0:T(8,128)(2,1)S(1)} %pad_maximum_fusion.own_ref), channel_id=1, source_target_pairs={{0,16},{16,32},{32,48},{48,256},{256,272},{272,288},{288,304},{1,1... | collective-permute-start | bytes 589832 | tf_op jit(solution)/shard_map/ppermute | solution.py:183
  2.3 2.9 %collective-permute-start = (bf16[128,384]{1,0:T(8,128)(2,1)}, bf16[128,384]{1,0:T(8,128)(2,1)S(1)}, u32[]{:S(2)}, u32[]{:S(2)}) collective-permute-start(bf16[128,384]{1,0:T(8,128)(2,1)} %bitcast.8), channel_id=1, source_target_pairs={{0,8},{8,0},{1,9},{9,1},{2,10},{10,2},{3,11},{11,3},{4,12},{12,4},... | collective-permute-start | bytes 294920 | tf_op jit(solution)/shard_map/ppermute | solution.py:180
  5.2 5.4 %collective-permute-start.5 = (bf16[128,768]{1,0:T(8,128)(2,1)S(1)}, bf16[128,768]{1,0:T(8,128)(2,1)S(1)}, u32[]{:S(2)}, u32[]{:S(2)}) collective-permute-start(bf16[128,768]{1,0:T(8,128)(2,1)S(1)} %pad_maximum_fusion.own_ref), channel_id=1, source_target_pairs={{0,304},{16,0},{32,16},{48,32},{272,256},{288,272},{304,288},{1,30... | collective-permute-start | bytes 589832 | tf_op jit(solution)/shard_map/ppermute | solution.py:185
  10.7 0.0 collective-permute-done
  10.7 5.0 %collective-permute-done.1.refs_0_ = bf16[128,768]{1,0:T(8,128)(2,1)S(1)} collective-permute-done((bf16[128,768]{1,0:T(8,128)(2,1)S(1)}, bf16[128,768]{1,0:T(8,128)(2,1)S(1)}, u32[]{:S(2)}, u32[]{:S(2)}) %collective-permute-start.1) | collective-permute-done | bytes 196640 | tf_op jit(solution)/shard_map/ppermute | solution.py:183
  15.7 1.3 %collective-permute-start.2 = (bf16[128,768]{1,0:T(8,128)(2,1)S(1)}, bf16[128,768]{1,0:T(8,128)(2,1)S(1)}, u32[]{:S(2)}, u32[]{:S(2)}) collective-permute-start(bf16[128,768]{1,0:T(8,128)(2,1)S(1)} %collective-permute-done.1.refs_0_), channel_id=1, source_target_pairs={{16,32},{32,48},{48,256},{256,272},{272,288},{288,304},{17,33},{33... | collective-permute-start | bytes 589832 | tf_op jit(solution)/shard_map/ppermute | solution.py:183
  17.0 0.9 pad_maximum_fusion.1
  17.9 0.9 broadcast_in_dim.4
  18.9 4.5 %all-to-all-start = ((bf16[4,256,384]{2,1,0:T(8,128)(2,1)}), bf16[4,256,384]{2,1,0:T(8,128)(2,1)S(1)}, u32[]{:S(2)}, u32[]{:S(2)}) async-start(bf16[4,256,384]{2,1,0:T(8,128)(2,1)} %broadcast_in_dim.4), calls=%async_computation | async-start | bytes 1572864 | tf_op jit(solution)/shard_map/all_to_all | solution.py:164
  23.3 0.0 collective-permute-done.5.refs_4_
  23.3 5.4 %collective-permute-start.6 = (bf16[128,768]{1,0:T(8,128)(2,1)S(1)}, bf16[128,768]{1,0:T(8,128)(2,1)S(1)}, u32[]{:S(2)}, u32[]{:S(2)}) collective-permute-start(bf16[128,768]{1,0:T(8,128)(2,1)S(1)} %collective-permute-done.5.refs_4_), channel_id=1, source_target_pairs={{0,304},{16,0},{32,16},{272,256},{288,272},{304,288},{1,305},{17,1... | collective-permute-start | bytes 589832 | tf_op jit(solution)/shard_map/ppermute | solution.py:185
  28.8 0.0 collective-permute-done.2.refs_1_
  28.8 1.3 %collective-permute-start.3 = (bf16[128,768]{1,0:T(8,128)(2,1)S(1)}, bf16[128,768]{1,0:T(8,128)(2,1)S(1)}, u32[]{:S(2)}, u32[]{:S(2)}) collective-permute-start(bf16[128,768]{1,0:T(8,128)(2,1)S(1)} %collective-permute-done.2.refs_1_), channel_id=1, source_target_pairs={{32,48},{48,256},{256,272},{272,288},{288,304},{33,49},{49,257},{2... | collective-permute-start | bytes 589832 | tf_op jit(solution)/shard_map/ppermute | solution.py:183
  30.1 5.4 %collective-permute-done.6.refs_5_ = bf16[128,768]{1,0:T(8,128)(2,1)S(1)} collective-permute-done((bf16[128,768]{1,0:T(8,128)(2,1)S(1)}, bf16[128,768]{1,0:T(8,128)(2,1)S(1)}, u32[]{:S(2)}, u32[]{:S(2)}) %collective-permute-start.6) | collective-permute-done | bytes 196640 | tf_op jit(solution)/shard_map/ppermute | solution.py:185
  35.5 5.1 %collective-permute-start.7 = (bf16[128,768]{1,0:T(8,128)(2,1)S(1)}, bf16[128,768]{1,0:T(8,128)(2,1)S(1)}, u32[]{:S(2)}, u32[]{:S(2)}) collective-permute-start(bf16[128,768]{1,0:T(8,128)(2,1)S(1)} %collective-permute-done.6.refs_5_), channel_id=1, source_target_pairs={{0,304},{16,0},{272,256},{288,272},{304,288},{1,305},{17,1},{273,2... | collective-permute-start | bytes 589832 | tf_op jit(solution)/shard_map/ppermute | solution.py:185
  40.6 0.0 collective-permute-done.3.refs_2_
  40.6 1.3 %collective-permute-start.4 = (bf16[128,768]{1,0:T(8,128)(2,1)S(1)}, bf16[128,768]{1,0:T(8,128)(2,1)S(1)}, u32[]{:S(2)}, u32[]{:S(2)}) collective-permute-start(bf16[128,768]{1,0:T(8,128)(2,1)S(1)} %collective-permute-done.3.refs_2_), channel_id=1, source_target_pairs={{48,256},{256,272},{272,288},{288,304},{49,257},{257,273},{273,289... | collective-permute-start | bytes 589832 | tf_op jit(solution)/shard_map/ppermute | solution.py:183
  41.9 6.3 %collective-permute-done.7.refs_6_ = bf16[128,768]{1,0:T(8,128)(2,1)S(1)} collective-permute-done((bf16[128,768]{1,0:T(8,128)(2,1)S(1)}, bf16[128,768]{1,0:T(8,128)(2,1)S(1)}, u32[]{:S(2)}, u32[]{:S(2)}) %collective-permute-start.7) | collective-permute-done | bytes 196640 | tf_op jit(solution)/shard_map/ppermute | solution.py:185
  48.1 6.1 %collective-permute-done.4.refs_3_ = bf16[128,768]{1,0:T(8,128)(2,1)S(1)} collective-permute-done((bf16[128,768]{1,0:T(8,128)(2,1)S(1)}, bf16[128,768]{1,0:T(8,128)(2,1)S(1)}, u32[]{:S(2)}, u32[]{:S(2)}) %collective-permute-start.4) | collective-permute-done | bytes 196640 | tf_op jit(solution)/shard_map/ppermute | solution.py:183
  54.2 0.0 all-to-all-done
  54.2 0.0 copy-start
  54.2 4.5 %shard_map.46 = bf16[8,400,128]{2,1,0:T(8,128)(2,1)S(1)} custom-call(bf16[1024,384]{1,0:T(8,128)(2,1)S(1)} %bitcast.5, bf16[128,768]{1,0:T(8,128)(2,1)S(1)} %pad_maximum_fusion.own_ref, bf16[128,768]{1,0:T(8,128)(2,1)S(1)} %collective-permute-done.1.refs_0_, bf16[128,768]{1,0:T(8,128)(2,1)S(1)} %collective-permute-done.2.refs_1_, ...), custom_call_target="tpu_custom_call" | custom-call | tf_op jit(solution)/shard_map/pallas_call | solution.py:95
  58.7 18.2 %all_to_all.15.parts_ref = bf16[8,400,128]{2,1,0:T(8,128)(2,1)S(1)} all-to-all(bf16[8,400,128]{2,1,0:T(8,128)(2,1)S(1)} %shard_map.46), channel_id=1, replica_groups=mesh['branch'=2,'y'=4,'z2'=2,'z1'=2,'z0'=2,'x'=4,'core'=2] {'y','z0'}, dimensions={0} | all-to-all | bytes 1638400 | tf_op jit(solution)/shard_map/all_to_all | solution.py:191
  76.9 0.0 copy-done
  76.9 1.4 %shard_map.47 = (bf16[4,128,384]{2,1,0:T(8,128)(2,1)S(1)}, bf16[4,128,384]{2,1,0:T(8,128)(2,1)S(1)}) custom-call(bf16[8,400,128]{2,1,0:T(8,128)(2,1)S(1)} %all_to_all.15.parts_ref, bf16[384,3072]{1,0:T(8,128)(2,1)S(1)} %copy-done), custom_call_target="tpu_custom_call" | custom-call | flops 301989888 | bytes 3178496 | tf_op jit(solution)/shard_map/pallas_call | solution.py:149
  78.2 1.9 %collective-permute-start.8 = (bf16[4,128,384]{2,1,0:T(8,128)(2,1)S(1)}, bf16[4,128,384]{2,1,0:T(8,128)(2,1)S(1)}, u32[]{:S(2)}, u32[]{:S(2)}) collective-permute-start(bf16[4,128,384]{2,1,0:T(8,128)(2,1)S(1)} %get-tuple-element.12), channel_id=1, source_target_pairs={{0,1},{1,0},{2,3},{3,2},{4,5},{5,4},{6,7},{7,6},{8,9},{9,8},{10,11... | collective-permute-start | bytes 1179656 | tf_op jit(solution)/shard_map/ppermute | solution.py:193
  80.2 1.7 %collective-permute-done.8 = bf16[4,128,384]{2,1,0:T(8,128)(2,1)S(1)} collective-permute-done((bf16[4,128,384]{2,1,0:T(8,128)(2,1)S(1)}, bf16[4,128,384]{2,1,0:T(8,128)(2,1)S(1)}, u32[]{:S(2)}, u32[]{:S(2)}) %collective-permute-start.8) | collective-permute-done | bytes 393248 | tf_op jit(solution)/shard_map/ppermute | solution.py:193
  81.8 0.1 add_convert_fusion
  82.0 12.5 %all_to_all.16 = bf16[4,128,384]{2,1,0:T(8,128)(2,1)S(1)} all-to-all(bf16[4,128,384]{2,1,0:T(8,128)(2,1)S(1)} %add_convert_fusion), channel_id=1, replica_groups=mesh['branch'=2,'y'=4,'z2'=2,'z1'=2,'z0'=2,'x'=4,'core'=2] {'x'}, dimensions={0} | all-to-all | bytes 786432 | tf_op jit(solution)/shard_map/all_to_all | solution.py:195
  94.4 0.7 reduce_sum.12
Async XLA Ops:
  1.0 14.7 %collective-permute-start.1 = (bf16[128,768]{1,0:T(8,128)(2,1)S(1)}, bf16[128,768]{1,0:T(8,128)(2,1)S(1)}, u32[]{:S(2)}, u32[]{:S(2)}) collective-permute-start(bf16[128,768]{1,0:T(8,128)(2,1)S(1)} %pad_maximum_fusion.own_ref), channel_id=1, source_target_pairs={{0,16},{16,32},{32,48},{48,256},{256,272},{272,288},{288,304},{1,1... | collective-permute-start | bytes 589832 | tf_op jit(solution)/shard_map/ppermute | solution.py:183
  2.3 8.4 %collective-permute-start = (bf16[128,384]{1,0:T(8,128)(2,1)}, bf16[128,384]{1,0:T(8,128)(2,1)S(1)}, u32[]{:S(2)}, u32[]{:S(2)}) collective-permute-start(bf16[128,384]{1,0:T(8,128)(2,1)} %bitcast.8), channel_id=1, source_target_pairs={{0,8},{8,0},{1,9},{9,1},{2,10},{10,2},{3,11},{11,3},{4,12},{12,4},... | collective-permute-start | bytes 294920 | tf_op jit(solution)/shard_map/ppermute | solution.py:180
  5.2 18.1 %collective-permute-start.5 = (bf16[128,768]{1,0:T(8,128)(2,1)S(1)}, bf16[128,768]{1,0:T(8,128)(2,1)S(1)}, u32[]{:S(2)}, u32[]{:S(2)}) collective-permute-start(bf16[128,768]{1,0:T(8,128)(2,1)S(1)} %pad_maximum_fusion.own_ref), channel_id=1, source_target_pairs={{0,304},{16,0},{32,16},{48,32},{272,256},{288,272},{304,288},{1,30... | collective-permute-start | bytes 589832 | tf_op jit(solution)/shard_map/ppermute | solution.py:185
  15.7 13.1 %collective-permute-start.2 = (bf16[128,768]{1,0:T(8,128)(2,1)S(1)}, bf16[128,768]{1,0:T(8,128)(2,1)S(1)}, u32[]{:S(2)}, u32[]{:S(2)}) collective-permute-start(bf16[128,768]{1,0:T(8,128)(2,1)S(1)} %collective-permute-done.1.refs_0_), channel_id=1, source_target_pairs={{16,32},{32,48},{48,256},{256,272},{272,288},{288,304},{17,33},{33... | collective-permute-start | bytes 589832 | tf_op jit(solution)/shard_map/ppermute | solution.py:183
  18.9 35.4 %all-to-all-start = ((bf16[4,256,384]{2,1,0:T(8,128)(2,1)}), bf16[4,256,384]{2,1,0:T(8,128)(2,1)S(1)}, u32[]{:S(2)}, u32[]{:S(2)}) async-start(bf16[4,256,384]{2,1,0:T(8,128)(2,1)} %broadcast_in_dim.4), calls=%async_computation | async-start | bytes 1572864 | tf_op jit(solution)/shard_map/all_to_all | solution.py:164
  23.3 12.1 %collective-permute-start.6 = (bf16[128,768]{1,0:T(8,128)(2,1)S(1)}, bf16[128,768]{1,0:T(8,128)(2,1)S(1)}, u32[]{:S(2)}, u32[]{:S(2)}) collective-permute-start(bf16[128,768]{1,0:T(8,128)(2,1)S(1)} %collective-permute-done.5.refs_4_), channel_id=1, source_target_pairs={{0,304},{16,0},{32,16},{272,256},{288,272},{304,288},{1,305},{17,1... | collective-permute-start | bytes 589832 | tf_op jit(solution)/shard_map/ppermute | solution.py:185
  28.8 11.8 %collective-permute-start.3 = (bf16[128,768]{1,0:T(8,128)(2,1)S(1)}, bf16[128,768]{1,0:T(8,128)(2,1)S(1)}, u32[]{:S(2)}, u32[]{:S(2)}) collective-permute-start(bf16[128,768]{1,0:T(8,128)(2,1)S(1)} %collective-permute-done.2.refs_1_), channel_id=1, source_target_pairs={{32,48},{48,256},{256,272},{272,288},{288,304},{33,49},{49,257},{2... | collective-permute-start | bytes 589832 | tf_op jit(solution)/shard_map/ppermute | solution.py:183
  35.5 12.7 %collective-permute-start.7 = (bf16[128,768]{1,0:T(8,128)(2,1)S(1)}, bf16[128,768]{1,0:T(8,128)(2,1)S(1)}, u32[]{:S(2)}, u32[]{:S(2)}) collective-permute-start(bf16[128,768]{1,0:T(8,128)(2,1)S(1)} %collective-permute-done.6.refs_5_), channel_id=1, source_target_pairs={{0,304},{16,0},{272,256},{288,272},{304,288},{1,305},{17,1},{273,2... | collective-permute-start | bytes 589832 | tf_op jit(solution)/shard_map/ppermute | solution.py:185
  40.6 13.7 %collective-permute-start.4 = (bf16[128,768]{1,0:T(8,128)(2,1)S(1)}, bf16[128,768]{1,0:T(8,128)(2,1)S(1)}, u32[]{:S(2)}, u32[]{:S(2)}) collective-permute-start(bf16[128,768]{1,0:T(8,128)(2,1)S(1)} %collective-permute-done.3.refs_2_), channel_id=1, source_target_pairs={{48,256},{256,272},{272,288},{288,304},{49,257},{257,273},{273,289... | collective-permute-start | bytes 589832 | tf_op jit(solution)/shard_map/ppermute | solution.py:183
  54.2 22.6 %copy-start = (bf16[384,3072]{1,0:T(8,128)(2,1)S(1)}, bf16[384,3072]{1,0:T(8,128)(2,1)}, u32[]{:S(2)}) copy-start(bf16[384,3072]{1,0:T(8,128)(2,1)} %weight_ref.1) | copy-start | bytes 7077892
  78.2 3.6 %collective-permute-start.8 = (bf16[4,128,384]{2,1,0:T(8,128)(2,1)S(1)}, bf16[4,128,384]{2,1,0:T(8,128)(2,1)S(1)}, u32[]{:S(2)}, u32[]{:S(2)}) collective-permute-start(bf16[4,128,384]{2,1,0:T(8,128)(2,1)S(1)} %get-tuple-element.12), channel_id=1, source_target_pairs={{0,1},{1,0},{2,3},{3,2},{4,5},{5,4},{6,7},{7,6},{8,9},{9,8},{10,11... | collective-permute-start | bytes 1179656 | tf_op jit(solution)/shard_map/ppermute | solution.py:193

commit v7 on v6

--- a/solution.py
+++ b/solution.py
@@ -101,7 +101,11 @@
             pltpu.VMEM((blocks, 8, BLOCK), jnp.float32),
         ],
         compiler_params=pltpu.CompilerParams(vmem_limit_bytes=32 * 1024 * 1024),
-        cost_estimate=pl.CostEstimate(flops=0, bytes_accessed=0, transcendentals=0),
+        cost_estimate=pl.CostEstimate(
+            flops=4 * rows * keys * feats,
+            bytes_accessed=2 * (2 * rows * feats + 2 * keys * feats),
+            transcendentals=rows * keys * heads,
+        ),
     )(queries, own, *up, *down)
 
 
@@ -184,7 +188,7 @@
         if step < 4:
             down.append(lax.ppermute(down[-1], KEY_AXES, ring_pairs(step, -1)))
         if step == 1:
-            beside, up[1] = lax.optimization_barrier((beside, up[1]))
+            beside = lax.optimization_barrier((beside, up[1]))[0]
             pair = jnp.concatenate([query, beside], axis=0)
             queries = spread(pair, "y").reshape(-1, query.shape[1])
     partial = attend(queries, own, up[1:], down[1:])

time: 95.6 us -> 95.6 us (level)
  no operation moved by 1% of the time
where the time goes in v7:
time: 95.6 us; the launch traced here: 95.1 us
  blocking collectives  30.6 us (32%)
  starting transfers between devices  30.4 us (32%)
  waiting for transfers between devices  24.5 us (26%)
  Pallas kernels  5.82 us (6%)
  other arithmetic  2.68 us (3%)
    all_to_all x1, blocking collectives, body(): lax.all_to_all(partial, ROW_AXES, split_axis=0, concat_axis=0, tiled=True)  18.2 us
    ppermute x3, starting transfers between devices, body(): down.append(lax.ppermute(down[-1], KEY_AXES, ring_pairs(step, -1)))  16 us
    all_to_all x1, blocking collectives, body(): lax.all_to_all(shares, 'x', split_axis=0, concat_axis=0, tiled=True)  12.5 us
    ppermute x3, waiting for transfers between devices, body(): down.append(lax.ppermute(down[-1], KEY_AXES, ring_pairs(step, -1)))  11.6 us
    ppermute x4, waiting for transfers between devices, body(): up.append(lax.ppermute(up[-1], KEY_AXES, ring_pairs(step, 1)))  11.1 us
    ppermute x4, starting transfers between devices, body(): up.append(lax.ppermute(up[-1], KEY_AXES, ring_pairs(step, 1)))  5.16 us
    all_to_all x1, starting transfers between devices, spread(): return lax.all_to_all(copies, axes, split_axis=0, concat_axis=0, tiled=True)  4.46 us
    pallas_call x1, Pallas kernels, attend(): pl.pallas_call(attend_kernel, out_shape=jax.ShapeDtypeStruct((blocks, hea...  4.46 us
  transfers between devices with their start and end apart: 10, of which 5 were waited for; matrix products, arithmetic and copies ran while one was open for 2% of the time, Pallas kernels for 0%

profile of v7, /device:TPU:448, one launch (start us, length us, event | category | flops | bytes accessed | tf_op | source)
XLA Modules:
  0.0 95.1 jit_solution(1581104044971533759)
XLA Ops:
  0.0 1.0 %pad_maximum_fusion.own_ref = bf16[128,768]{1,0:T(8,128)(2,1)S(1)} fusion(bf16[128,384]{1,0:T(8,128)(2,1)} %bitcast.6, bf16[128,384]{1,0:T(8,128)(2,1)} %bitcast.7), kind=kLoop, calls=%fused_computation.1 | loop fusion | flops 393216 | bytes 393216 | tf_op jit(solution)/shard_map/concatenate | solution.py:182
  1.0 1.3 %collective-permute-start.1 = (bf16[128,768]{1,0:T(8,128)(2,1)S(1)}, bf16[128,768]{1,0:T(8,128)(2,1)S(1)}, u32[]{:S(2)}, u32[]{:S(2)}) collective-permute-start(bf16[128,768]{1,0:T(8,128)(2,1)S(1)} %pad_maximum_fusion.own_ref), channel_id=1, source_target_pairs={{0,16},{16,32},{32,48},{48,256},{256,272},{272,288},{288,304},{1,1... | collective-permute-start | bytes 589832 | tf_op jit(solution)/shard_map/ppermute | solution.py:187
  2.3 2.9 %collective-permute-start = (bf16[128,384]{1,0:T(8,128)(2,1)}, bf16[128,384]{1,0:T(8,128)(2,1)S(1)}, u32[]{:S(2)}, u32[]{:S(2)}) collective-permute-start(bf16[128,384]{1,0:T(8,128)(2,1)} %bitcast.8), channel_id=1, source_target_pairs={{0,8},{8,0},{1,9},{9,1},{2,10},{10,2},{3,11},{11,3},{4,12},{12,4},... | collective-permute-start | bytes 294920 | tf_op jit(solution)/shard_map/ppermute | solution.py:184
  5.2 5.4 %collective-permute-start.5 = (bf16[128,768]{1,0:T(8,128)(2,1)S(1)}, bf16[128,768]{1,0:T(8,128)(2,1)S(1)}, u32[]{:S(2)}, u32[]{:S(2)}) collective-permute-start(bf16[128,768]{1,0:T(8,128)(2,1)S(1)} %pad_maximum_fusion.own_ref), channel_id=1, source_target_pairs={{0,304},{16,0},{32,16},{48,32},{272,256},{288,272},{304,288},{1,30... | collective-permute-start | bytes 589832 | tf_op jit(solution)/shard_map/ppermute | solution.py:189
  10.7 0.0 collective-permute-done
  10.7 5.0 %collective-permute-done.1.refs_0_ = bf16[128,768]{1,0:T(8,128)(2,1)S(1)} collective-permute-done((bf16[128,768]{1,0:T(8,128)(2,1)S(1)}, bf16[128,768]{1,0:T(8,128)(2,1)S(1)}, u32[]{:S(2)}, u32[]{:S(2)}) %collective-permute-start.1) | collective-permute-done | bytes 196640 | tf_op jit(solution)/shard_map/ppermute | solution.py:187
  15.7 1.3 %collective-permute-start.2 = (bf16[128,768]{1,0:T(8,128)(2,1)S(1)}, bf16[128,768]{1,0:T(8,128)(2,1)S(1)}, u32[]{:S(2)}, u32[]{:S(2)}) collective-permute-start(bf16[128,768]{1,0:T(8,128)(2,1)S(1)} %collective-permute-done.1.refs_0_), channel_id=1, source_target_pairs={{16,32},{32,48},{48,256},{256,272},{272,288},{288,304},{17,33},{33... | collective-permute-start | bytes 589832 | tf_op jit(solution)/shard_map/ppermute | solution.py:187
  17.0 0.9 pad_maximum_fusion.1
  17.9 0.9 broadcast_in_dim.4
  18.9 4.5 %all-to-all-start = ((bf16[4,256,384]{2,1,0:T(8,128)(2,1)}), bf16[4,256,384]{2,1,0:T(8,128)(2,1)S(1)}, u32[]{:S(2)}, u32[]{:S(2)}) async-start(bf16[4,256,384]{2,1,0:T(8,128)(2,1)} %broadcast_in_dim.4), calls=%async_computation | async-start | bytes 1572864 | tf_op jit(solution)/shard_map/all_to_all | solution.py:168
  23.3 0.0 collective-permute-done.5.refs_4_
  23.3 5.4 %collective-permute-start.6 = (bf16[128,768]{1,0:T(8,128)(2,1)S(1)}, bf16[128,768]{1,0:T(8,128)(2,1)S(1)}, u32[]{:S(2)}, u32[]{:S(2)}) collective-permute-start(bf16[128,768]{1,0:T(8,128)(2,1)S(1)} %collective-permute-done.5.refs_4_), channel_id=1, source_target_pairs={{0,304},{16,0},{32,16},{272,256},{288,272},{304,288},{1,305},{17,1... | collective-permute-start | bytes 589832 | tf_op jit(solution)/shard_map/ppermute | solution.py:189
  28.8 0.0 collective-permute-done.2.refs_1_
  28.8 1.3 %collective-permute-start.3 = (bf16[128,768]{1,0:T(8,128)(2,1)S(1)}, bf16[128,768]{1,0:T(8,128)(2,1)S(1)}, u32[]{:S(2)}, u32[]{:S(2)}) collective-permute-start(bf16[128,768]{1,0:T(8,128)(2,1)S(1)} %collective-permute-done.2.refs_1_), channel_id=1, source_target_pairs={{32,48},{48,256},{256,272},{272,288},{288,304},{33,49},{49,257},{2... | collective-permute-start | bytes 589832 | tf_op jit(solution)/shard_map/ppermute | solution.py:187
  30.1 5.4 %collective-permute-done.6.refs_5_ = bf16[128,768]{1,0:T(8,128)(2,1)S(1)} collective-permute-done((bf16[128,768]{1,0:T(8,128)(2,1)S(1)}, bf16[128,768]{1,0:T(8,128)(2,1)S(1)}, u32[]{:S(2)}, u32[]{:S(2)}) %collective-permute-start.6) | collective-permute-done | bytes 196640 | tf_op jit(solution)/shard_map/ppermute | solution.py:189
  35.5 5.1 %collective-permute-start.7 = (bf16[128,768]{1,0:T(8,128)(2,1)S(1)}, bf16[128,768]{1,0:T(8,128)(2,1)S(1)}, u32[]{:S(2)}, u32[]{:S(2)}) collective-permute-start(bf16[128,768]{1,0:T(8,128)(2,1)S(1)} %collective-permute-done.6.refs_5_), channel_id=1, source_target_pairs={{0,304},{16,0},{272,256},{288,272},{304,288},{1,305},{17,1},{273,2... | collective-permute-start | bytes 589832 | tf_op jit(solution)/shard_map/ppermute | solution.py:189
  40.6 0.0 collective-permute-done.3.refs_2_
  40.6 1.3 %collective-permute-start.4 = (bf16[128,768]{1,0:T(8,128)(2,1)S(1)}, bf16[128,768]{1,0:T(8,128)(2,1)S(1)}, u32[]{:S(2)}, u32[]{:S(2)}) collective-permute-start(bf16[128,768]{1,0:T(8,128)(2,1)S(1)} %collective-permute-done.3.refs_2_), channel_id=1, source_target_pairs={{48,256},{256,272},{272,288},{288,304},{49,257},{257,273},{273,289... | collective-permute-start | bytes 589832 | tf_op jit(solution)/shard_map/ppermute | solution.py:187
  41.9 6.3 %collective-permute-done.7.refs_6_ = bf16[128,768]{1,0:T(8,128)(2,1)S(1)} collective-permute-done((bf16[128,768]{1,0:T(8,128)(2,1)S(1)}, bf16[128,768]{1,0:T(8,128)(2,1)S(1)}, u32[]{:S(2)}, u32[]{:S(2)}) %collective-permute-start.7) | collective-permute-done | bytes 196640 | tf_op jit(solution)/shard_map/ppermute | solution.py:189
  48.1 6.1 %collective-permute-done.4.refs_3_ = bf16[128,768]{1,0:T(8,128)(2,1)S(1)} collective-permute-done((bf16[128,768]{1,0:T(8,128)(2,1)S(1)}, bf16[128,768]{1,0:T(8,128)(2,1)S(1)}, u32[]{:S(2)}, u32[]{:S(2)}) %collective-permute-start.4) | collective-permute-done | bytes 196640 | tf_op jit(solution)/shard_map/ppermute | solution.py:187
  54.2 0.0 all-to-all-done
  54.2 0.0 copy-start
  54.2 4.5 %shard_map.46 = bf16[8,400,128]{2,1,0:T(8,128)(2,1)S(1)} custom-call(bf16[1024,384]{1,0:T(8,128)(2,1)S(1)} %bitcast.5, bf16[128,768]{1,0:T(8,128)(2,1)S(1)} %pad_maximum_fusion.own_ref, bf16[128,768]{1,0:T(8,128)(2,1)S(1)} %collective-permute-done.1.refs_0_, bf16[128,768]{1,0:T(8,128)(2,1)S(1)} %collective-permute-done.2.refs_1_, ...), custom_call_target="tpu_custom_call" | custom-call | flops 1610612736 | bytes 3145728 | tf_op jit(solution)/shard_map/pallas_call | solution.py:95
  58.7 18.2 %all_to_all.15.parts_ref = bf16[8,400,128]{2,1,0:T(8,128)(2,1)S(1)} all-to-all(bf16[8,400,128]{2,1,0:T(8,128)(2,1)S(1)} %shard_map.46), channel_id=1, replica_groups=mesh['branch'=2,'y'=4,'z2'=2,'z1'=2,'z0'=2,'x'=4,'core'=2] {'y','z0'}, dimensions={0} | all-to-all | bytes 1638400 | tf_op jit(solution)/shard_map/all_to_all | solution.py:195
  76.9 0.0 copy-done
  76.9 1.4 %shard_map.47 = (bf16[4,128,384]{2,1,0:T(8,128)(2,1)S(1)}, bf16[4,128,384]{2,1,0:T(8,128)(2,1)S(1)}) custom-call(bf16[8,400,128]{2,1,0:T(8,128)(2,1)S(1)} %all_to_all.15.parts_ref, bf16[384,3072]{1,0:T(8,128)(2,1)S(1)} %copy-done), custom_call_target="tpu_custom_call" | custom-call | flops 301989888 | bytes 3178496 | tf_op jit(solution)/shard_map/pallas_call | solution.py:153
  78.2 1.9 %collective-permute-start.8 = (bf16[4,128,384]{2,1,0:T(8,128)(2,1)S(1)}, bf16[4,128,384]{2,1,0:T(8,128)(2,1)S(1)}, u32[]{:S(2)}, u32[]{:S(2)}) collective-permute-start(bf16[4,128,384]{2,1,0:T(8,128)(2,1)S(1)} %get-tuple-element.10), channel_id=1, source_target_pairs={{0,1},{1,0},{2,3},{3,2},{4,5},{5,4},{6,7},{7,6},{8,9},{9,8},{10,11... | collective-permute-start | bytes 1179656 | tf_op jit(solution)/shard_map/ppermute | solution.py:197
  80.2 1.7 %collective-permute-done.8 = bf16[4,128,384]{2,1,0:T(8,128)(2,1)S(1)} collective-permute-done((bf16[4,128,384]{2,1,0:T(8,128)(2,1)S(1)}, bf16[4,128,384]{2,1,0:T(8,128)(2,1)S(1)}, u32[]{:S(2)}, u32[]{:S(2)}) %collective-permute-start.8) | collective-permute-done | bytes 393248 | tf_op jit(solution)/shard_map/ppermute | solution.py:197
  81.8 0.1 add_convert_fusion
  82.0 12.5 %all_to_all.16 = bf16[4,128,384]{2,1,0:T(8,128)(2,1)S(1)} all-to-all(bf16[4,128,384]{2,1,0:T(8,128)(2,1)S(1)} %add_convert_fusion), channel_id=1, replica_groups=mesh['branch'=2,'y'=4,'z2'=2,'z1'=2,'z0'=2,'x'=4,'core'=2] {'x'}, dimensions={0} | all-to-all | bytes 786432 | tf_op jit(solution)/shard_map/all_to_all | solution.py:199
  94.4 0.7 reduce_sum.12
Async XLA Ops:
  1.0 14.7 %collective-permute-start.1 = (bf16[128,768]{1,0:T(8,128)(2,1)S(1)}, bf16[128,768]{1,0:T(8,128)(2,1)S(1)}, u32[]{:S(2)}, u32[]{:S(2)}) collective-permute-start(bf16[128,768]{1,0:T(8,128)(2,1)S(1)} %pad_maximum_fusion.own_ref), channel_id=1, source_target_pairs={{0,16},{16,32},{32,48},{48,256},{256,272},{272,288},{288,304},{1,1... | collective-permute-start | bytes 589832 | tf_op jit(solution)/shard_map/ppermute | solution.py:187
  2.3 8.4 %collective-permute-start = (bf16[128,384]{1,0:T(8,128)(2,1)}, bf16[128,384]{1,0:T(8,128)(2,1)S(1)}, u32[]{:S(2)}, u32[]{:S(2)}) collective-permute-start(bf16[128,384]{1,0:T(8,128)(2,1)} %bitcast.8), channel_id=1, source_target_pairs={{0,8},{8,0},{1,9},{9,1},{2,10},{10,2},{3,11},{11,3},{4,12},{12,4},... | collective-permute-start | bytes 294920 | tf_op jit(solution)/shard_map/ppermute | solution.py:184
  5.2 18.1 %collective-permute-start.5 = (bf16[128,768]{1,0:T(8,128)(2,1)S(1)}, bf16[128,768]{1,0:T(8,128)(2,1)S(1)}, u32[]{:S(2)}, u32[]{:S(2)}) collective-permute-start(bf16[128,768]{1,0:T(8,128)(2,1)S(1)} %pad_maximum_fusion.own_ref), channel_id=1, source_target_pairs={{0,304},{16,0},{32,16},{48,32},{272,256},{288,272},{304,288},{1,30... | collective-permute-start | bytes 589832 | tf_op jit(solution)/shard_map/ppermute | solution.py:189
  15.7 13.1 %collective-permute-start.2 = (bf16[128,768]{1,0:T(8,128)(2,1)S(1)}, bf16[128,768]{1,0:T(8,128)(2,1)S(1)}, u32[]{:S(2)}, u32[]{:S(2)}) collective-permute-start(bf16[128,768]{1,0:T(8,128)(2,1)S(1)} %collective-permute-done.1.refs_0_), channel_id=1, source_target_pairs={{16,32},{32,48},{48,256},{256,272},{272,288},{288,304},{17,33},{33... | collective-permute-start | bytes 589832 | tf_op jit(solution)/shard_map/ppermute | solution.py:187
  18.9 35.4 %all-to-all-start = ((bf16[4,256,384]{2,1,0:T(8,128)(2,1)}), bf16[4,256,384]{2,1,0:T(8,128)(2,1)S(1)}, u32[]{:S(2)}, u32[]{:S(2)}) async-start(bf16[4,256,384]{2,1,0:T(8,128)(2,1)} %broadcast_in_dim.4), calls=%async_computation | async-start | bytes 1572864 | tf_op jit(solution)/shard_map/all_to_all | solution.py:168
  23.3 12.1 %collective-permute-start.6 = (bf16[128,768]{1,0:T(8,128)(2,1)S(1)}, bf16[128,768]{1,0:T(8,128)(2,1)S(1)}, u32[]{:S(2)}, u32[]{:S(2)}) collective-permute-start(bf16[128,768]{1,0:T(8,128)(2,1)S(1)} %collective-permute-done.5.refs_4_), channel_id=1, source_target_pairs={{0,304},{16,0},{32,16},{272,256},{288,272},{304,288},{1,305},{17,1... | collective-permute-start | bytes 589832 | tf_op jit(solution)/shard_map/ppermute | solution.py:189
  28.8 11.8 %collective-permute-start.3 = (bf16[128,768]{1,0:T(8,128)(2,1)S(1)}, bf16[128,768]{1,0:T(8,128)(2,1)S(1)}, u32[]{:S(2)}, u32[]{:S(2)}) collective-permute-start(bf16[128,768]{1,0:T(8,128)(2,1)S(1)} %collective-permute-done.2.refs_1_), channel_id=1, source_target_pairs={{32,48},{48,256},{256,272},{272,288},{288,304},{33,49},{49,257},{2... | collective-permute-start | bytes 589832 | tf_op jit(solution)/shard_map/ppermute | solution.py:187
  35.5 12.7 %collective-permute-start.7 = (bf16[128,768]{1,0:T(8,128)(2,1)S(1)}, bf16[128,768]{1,0:T(8,128)(2,1)S(1)}, u32[]{:S(2)}, u32[]{:S(2)}) collective-permute-start(bf16[128,768]{1,0:T(8,128)(2,1)S(1)} %collective-permute-done.6.refs_5_), channel_id=1, source_target_pairs={{0,304},{16,0},{272,256},{288,272},{304,288},{1,305},{17,1},{273,2... | collective-permute-start | bytes 589832 | tf_op jit(solution)/shard_map/ppermute | solution.py:189
  40.6 13.7 %collective-permute-start.4 = (bf16[128,768]{1,0:T(8,128)(2,1)S(1)}, bf16[128,768]{1,0:T(8,128)(2,1)S(1)}, u32[]{:S(2)}, u32[]{:S(2)}) collective-permute-start(bf16[128,768]{1,0:T(8,128)(2,1)S(1)} %collective-permute-done.3.refs_2_), channel_id=1, source_target_pairs={{48,256},{256,272},{272,288},{288,304},{49,257},{257,273},{273,289... | collective-permute-start | bytes 589832 | tf_op jit(solution)/shard_map/ppermute | solution.py:187
  54.2 22.6 %copy-start = (bf16[384,3072]{1,0:T(8,128)(2,1)S(1)}, bf16[384,3072]{1,0:T(8,128)(2,1)}, u32[]{:S(2)}) copy-start(bf16[384,3072]{1,0:T(8,128)(2,1)} %weight_ref.1) | copy-start | bytes 7077892
  78.2 3.6 %collective-permute-start.8 = (bf16[4,128,384]{2,1,0:T(8,128)(2,1)S(1)}, bf16[4,128,384]{2,1,0:T(8,128)(2,1)S(1)}, u32[]{:S(2)}, u32[]{:S(2)}) collective-permute-start(bf16[4,128,384]{2,1,0:T(8,128)(2,1)S(1)} %get-tuple-element.10), channel_id=1, source_target_pairs={{0,1},{1,0},{2,3},{3,2},{4,5},{5,4},{6,7},{7,6},{8,9},{9,8},{10,11... | collective-permute-start | bytes 1179656 | tf_op jit(solution)/shard_map/ppermute | solution.py:197
